TPU v7x, 32 devices: a whole 2x2x4 slice. The times are simulated.
32 devices in a mesh: dp: 4 (over z), head: 2 (over x), srv: 4 (over y, core).
Axes of the slice: x: 2, y: 2, z: 4, core: 2. Of those that a mesh axis runs over, the one named last changes fastest.
Arguments:
- queries: bfloat16 [512, 8, 1024], P('dp', 'srv', 'head'), may hold values from -5 to 5
- keys: bfloat16 [2560, 1024], P(('dp', 'head')), may hold values from -5 to 5
- values: bfloat16 [2560, 1024], P(('dp', 'head')), may hold values from -6 to 6
- output_gradient: bfloat16 [512, 8, 1024], P('dp', 'srv', 'head'), may hold values from -6 to 6
- doc_ids: int32 [2560], P('dp'), may hold values from 0 to 7, never falling along the last dimension, each value on 1 to 1280 neighbouring positions
Outputs:
- attention: bfloat16 [512, 8, 1024], P('dp', 'srv', 'head')
- q_grad: bfloat16 [512, 8, 1024], P('dp', 'srv', 'head')
- k_grad: bfloat16 [2560, 1024], P(('dp', 'head', 'srv'))
- v_grad: bfloat16 [2560, 1024], P(('dp', 'head', 'srv'))
Inputs may be any that keep to these rules, and one draw needn't show every extreme that they name: `doc_ids`: document numbers never fall along the keys; every document holds at most 1280 keys, and one holds exactly 1280.
All inputs are finite; a program needn't handle non-finite values.
Results may differ from a plain program's by a relative error of at most 0.039.
Values may be sent and summed in bfloat16 or wider, within the bound.
A program may use at most 64 MiB of HBM per device.

v0:
```python
import math

import jax
import jax.numpy as jnp
from jax import lax
from jax.sharding import PartitionSpec as P

HEAD_SIZE = 128


NEGATIVE = -1e30


def local(queries, keys, values, output_gradient, doc_ids):
    home_rows, pair_heads, group_width = queries.shape
    groups = group_width // HEAD_SIZE
    scale_factor = HEAD_SIZE ** (-0.5)
    key_rows, value_rows = (
        lax.all_to_all(keys, "head", split_axis=1, concat_axis=0, tiled=True),
        lax.all_to_all(values, "head", split_axis=1, concat_axis=0, tiled=True),
    )
    key_count = key_rows.shape[0]
    servers = lax.axis_size("dp")
    server = lax.axis_index("dp")
    key_at = server * key_count + jnp.arange(key_count, dtype=jnp.int32)
    all_docs = lax.all_gather(doc_ids, "dp", axis=0, tiled=True)
    query_total = home_rows * servers
    context = all_docs.shape[0] - query_total
    query_docs = all_docs[context:]
    query_places = context + jnp.arange(query_total, dtype=jnp.int32)
    all_q, all_dout = (
        lax.all_gather(queries, "dp", axis=0, tiled=True),
        lax.all_gather(output_gradient, "dp", axis=0, tiled=True),
    )
    block_rows = math.gcd(512, query_total)
    block_count = query_total // block_rows
    key_heads = key_rows.reshape(key_count, groups, HEAD_SIZE)
    value_heads = value_rows.reshape(key_count, groups, HEAD_SIZE)
    query_blocks = all_q.reshape(block_count, block_rows, pair_heads, groups, HEAD_SIZE)
    grad_blocks = all_dout.reshape(block_count, block_rows, pair_heads, groups, HEAD_SIZE)
    place_blocks = query_places.reshape(block_count, block_rows)
    doc_blocks = query_docs.reshape(block_count, block_rows)

    def admissible(places, query_doc):
        return (key_at[None, :] <= places[:, None]) & (doc_ids[None, :] == query_doc[:, None])

    def scores_of(query_block):
        return (
            jnp.einsum("pjgd,kgd->gjpk", query_block, key_heads, preferred_element_type=jnp.float32)
            * scale_factor
        )

    def block_max(inputs):
        query_block, places, query_doc = inputs
        allowed = admissible(places, query_doc)

        def compute():
            raw_scores = scores_of(query_block)
            masked = jnp.where(allowed[None, None], raw_scores, NEGATIVE)
            return (jnp.max(masked, axis=-1).transpose(2, 1, 0), raw_scores)

        return compute()

    def block_top(inputs):
        return block_max(inputs)[0]

    local_max = lax.map(block_top, (query_blocks, place_blocks, doc_blocks))
    row_max = lax.pmax(local_max.reshape(query_total, pair_heads, groups), "dp")
    max_blocks = row_max.reshape(block_count, block_rows, pair_heads, groups)

    def block_sum(inputs):
        stored, places, query_doc, row_top = inputs
        allowed = admissible(places, query_doc)

        def compute():
            block_scores = scores_of(stored)
            shifted = block_scores - row_top.transpose(2, 1, 0)[..., None]
            weights = jnp.where(allowed[None, None], jnp.exp(shifted), 0.0)
            weighted = jnp.einsum(
                "gjpk,kgd->pjgd",
                weights.astype(jnp.bfloat16),
                value_heads,
                preferred_element_type=jnp.float32,
            )
            return (
                weighted.reshape(block_rows, pair_heads, group_width),
                jnp.sum(weights, axis=-1).transpose(2, 1, 0),
            )

        return compute()

    part_out, part_norm = lax.map(block_sum, (query_blocks, place_blocks, doc_blocks, max_blocks))
    part_out = part_out.reshape(query_total, pair_heads, group_width)
    part_norm = part_norm.reshape(query_total, pair_heads, groups)
    home_out, home_norm = (
        lax.psum_scatter(part_out, "dp", scatter_dimension=0, tiled=True),
        lax.psum_scatter(part_norm, "dp", scatter_dimension=0, tiled=True),
    )
    home_max = lax.dynamic_slice_in_dim(row_max, server * home_rows, home_rows, 0)
    attn_home = (
        home_out.reshape(home_rows, pair_heads, groups, HEAD_SIZE) / home_norm[..., None]
    ).astype(jnp.bfloat16)
    log_home = home_max + jnp.log(home_norm)
    grad_home = output_gradient.reshape(home_rows, pair_heads, groups, HEAD_SIZE).astype(
        jnp.float32
    )
    delta_home = jnp.sum(grad_home * attn_home.astype(jnp.float32), axis=-1)
    log_all, delta_all = (
        lax.all_gather(log_home, "dp", axis=0, tiled=True),
        lax.all_gather(delta_home, "dp", axis=0, tiled=True),
    )
    attention = attn_home.reshape(home_rows, pair_heads, group_width)
    log_blocks = log_all.reshape(block_count, block_rows, pair_heads, groups)
    delta_blocks = delta_all.reshape(block_count, block_rows, pair_heads, groups)

    def block_grad(totals, inputs):
        query_block, grad_block, places, query_doc, log_norm, row_delta = inputs
        allowed = admissible(places, query_doc)

        def compute():
            shifted = scores_of(query_block) - log_norm.transpose(2, 1, 0)[..., None]
            probs = jnp.where(allowed[None, None], jnp.exp(shifted), 0.0)
            value_grad = jnp.einsum(
                "gjpk,pjgd->kgd",
                probs.astype(jnp.bfloat16),
                grad_block,
                preferred_element_type=jnp.float32,
            )
            weight_grad = jnp.einsum(
                "pjgd,kgd->gjpk", grad_block, value_heads, preferred_element_type=jnp.float32
            )
            score_grad = (probs * (weight_grad - row_delta.transpose(2, 1, 0)[..., None])).astype(
                jnp.bfloat16
            )
            query_grad = (
                jnp.einsum(
                    "gjpk,kgd->pjgd", score_grad, key_heads, preferred_element_type=jnp.float32
                )
                * scale_factor
            )
            key_grad = (
                jnp.einsum(
                    "gjpk,pjgd->kgd", score_grad, query_block, preferred_element_type=jnp.float32
                )
                * scale_factor
            )
            return (query_grad.reshape(block_rows, pair_heads, group_width), key_grad, value_grad)

        query_grad, key_grad, value_grad = compute()
        return ((totals[0] + key_grad, totals[1] + value_grad), query_grad)

    zero_start = jnp.zeros((key_count, groups, HEAD_SIZE), jnp.float32)
    grad_inputs = (query_blocks, grad_blocks, place_blocks, doc_blocks, log_blocks, delta_blocks)
    (key_total, value_total), query_parts = lax.scan(
        block_grad, (zero_start, zero_start), grad_inputs
    )
    q_summed = lax.psum_scatter(
        query_parts.reshape(query_total, pair_heads, group_width).astype(jnp.bfloat16),
        "dp",
        scatter_dimension=0,
        tiled=True,
    )
    spread_key, spread_value = (
        lax.all_to_all(
            key_total.reshape(key_count, group_width).astype(jnp.bfloat16),
            "head",
            split_axis=0,
            concat_axis=1,
            tiled=True,
        ).astype(jnp.float32),
        lax.all_to_all(
            value_total.reshape(key_count, group_width).astype(jnp.bfloat16),
            "head",
            split_axis=0,
            concat_axis=1,
            tiled=True,
        ).astype(jnp.float32),
    )
    k_summed, v_summed = (
        lax.psum_scatter(
            spread_key.astype(jnp.bfloat16), "srv", scatter_dimension=0, tiled=True
        ).astype(jnp.float32),
        lax.psum_scatter(
            spread_value.astype(jnp.bfloat16), "srv", scatter_dimension=0, tiled=True
        ).astype(jnp.float32),
    )
    return (attention, q_summed, k_summed.astype(jnp.bfloat16), v_summed.astype(jnp.bfloat16))


def solution(mesh):
    placed = (
        P("dp", "srv", "head"),
        P(("dp", "head"), None),
        P(("dp", "head"), None),
        P("dp", "srv", "head"),
        P("dp"),
    )
    return jax.shard_map(
        local,
        mesh=mesh,
        in_specs=placed,
        out_specs=(
            P("dp", "srv", "head"),
            P("dp", "srv", "head"),
            P(("dp", "head", "srv"), None),
            P(("dp", "head", "srv"), None),
        ),
        check_vma=False,
    )
```

profile of v0, /device:TPU:13, one launch (start us, length us, event | category | flops | bytes accessed | tf_op | source)
XLA Modules:
  0.0 259.9 jit_solution(13084274748653265240)
XLA Ops:
  7.2 1.8 copy.62
  9.1 2.0 copy.138
  11.0 3.5 %all-to-all-start = ((bf16[320,2,512]{2,0,1:T(8,128)(2,1)}), bf16[320,2,512]{2,0,1:T(8,128)(2,1)S(1)}, u32[]{:S(2)}, u32[]{:S(2)}) async-start(bf16[320,2,512]{2,0,1:T(8,128)(2,1)} %bitcast.108), calls=%async_computation | async-start | bytes 1310720 | tf_op jit(solution)/shard_map/all_to_all | solution.py:19
  15.3 10.9 %all-gather = s32[4,1,640]{2,1,0:T(1,128)S(1)} all-gather(s32[1,1,640]{2,1,0:T(1,128)S(1)} %reshape.147), channel_id=1, replica_groups=mesh['dp'=4,'head'=2,'srv'=4] {'dp'}, dimensions={0}, use_global_device_ids=true | all-gather | bytes 12800 | tf_op jit(solution)/shard_map/all_gather | solution.py:26
  26.2 2.0 copy.139
  28.2 3.5 %all-to-all-start.1 = ((bf16[320,2,512]{2,0,1:T(8,128)(2,1)}), bf16[320,2,512]{2,0,1:T(8,128)(2,1)S(1)}, u32[]{:S(2)}, u32[]{:S(2)}) async-start(bf16[320,2,512]{2,0,1:T(8,128)(2,1)} %bitcast.109), calls=%async_computation.1 | async-start | bytes 1310720 | tf_op jit(solution)/shard_map/all_to_all | solution.py:20
  33.9 4.4 %all-to-all-done.1 = bf16[320,2,512]{2,0,1:T(8,128)(2,1)S(1)} async-done(((bf16[320,2,512]{2,0,1:T(8,128)(2,1)}), bf16[320,2,512]{2,0,1:T(8,128)(2,1)S(1)}, u32[]{:S(2)}, u32[]{:S(2)}) %all-to-all-start.1) | async-done | bytes 655392 | tf_op jit(solution)/shard_map/all_to_all | solution.py:20
  39.6 7.2 %fusion.2 = (f32[4,2,512]{2,1,0:T(2,128)S(1)}, f32[4,640,512,2]{2,1,3,0:T(8,128)}) fusion(pred[512,640]{0,1:T(8,128)(4,1)S(1)} %compare_and_fusion, bf16[640,4,128,1]{0,2,3,1:T(8,128)(2,1)S(1)} %copy.93, bf16[512,2,4,128]{0,3,2,1:T(8,128)(2,1)} %bitcast.122), kind=kOutput, calls=%fused_computation.6 | convolution fusion | flops 678948864 | bytes 12533760 | tf_op jit(solution)/shard_map/while/body/eval_jaxpr/pjgd,kgd->gjpk/dot_general | solution.py:49
  46.8 11.5 %pmax.7 = f32[512,2,4]{0,1,2:T(2,128)S(1)} all-reduce(f32[512,2,4]{0,1,2:T(2,128)S(1)} %bitcast.132), channel_id=1, replica_groups=mesh['dp'=4,'head'=2,'srv'=4] {'dp'}, use_global_device_ids=true, to_apply=%region_1.2 | all-reduce | flops 4096 | bytes 32768 | tf_op jit(solution)/shard_map/pmax | solution.py:68
  58.3 6.1 %fusion.8 = f32[4,2,512]{2,1,0:T(2,128)S(1)} fusion(f32[4,640,512,2]{2,1,3,0:T(8,128)} %get-tuple-element.88, f32[4,2,512]{2,1,0:T(2,128)S(1)} %bitcast.129, pred[512,640]{0,1:T(8,128)(4,1)S(1)} %compare_and_fusion), kind=kLoop, calls=%fused_computation.12 | loop fusion | flops 10481664 | bytes 10846208 | tf_op jit(solution)/shard_map/while/body/eval_jaxpr/reduce_sum | solution.py:87
  66.2 6.3 %fusion.16 = f32[512,2,4,128]{0,3,1,2:T(8,128)S(1)} fusion(f32[4,640,512,2]{2,1,3,0:T(8,128)} %get-tuple-element.88, f32[4,2,512]{2,1,0:T(2,128)S(1)} %bitcast.130, pred[512,640]{0,1:T(8,128)(4,1)S(1)} %compare_and_fusion, bf16[640,4,128,1]{2,1,0,3:T(4,128)(2,1)S(1)} %bitcast.127), kind=kOutput, calls=%fused_computation.19 | convolution fusion | flops 681574400 | bytes 13582336 | tf_op jit(solution)/shard_map/while/body/eval_jaxpr/gjpk,kgd->pjgd/dot_general | solution.py:79
  72.4 1.5 copy.68
  75.2 12.9 %reduce-scatter.16.cloned.1.call-done = f32[128,8]{1,0:T(8,128)} async-done(((f32[512,8]{1,0:T(8,128)}), f32[128,8]{1,0:T(8,128)}) %reduce-scatter.16.cloned.1.call-update) | async-done | bytes 4112
  89.3 8.7 %all_gather.17 = f32[512,2,4]{0,1,2:T(2,128)S(1)} all-gather(f32[128,2,4]{0,1,2:T(2,128)S(1)} %log_add_fusion), channel_id=1, replica_groups=mesh['dp'=4,'head'=2,'srv'=4] {'dp'}, dimensions={0}, use_global_device_ids=true | all-gather | bytes 20480 | tf_op jit(solution)/shard_map/all_gather | solution.py:109
  98.1 36.3 %reduce-scatter.10.cloned.1.call-done = f32[128,2,512]{0,2,1:T(8,128)} async-done(((f32[512,2,512]{0,2,1:T(8,128)}), f32[128,2,512]{0,2,1:T(8,128)}) %reduce-scatter.10.cloned.1.call-update) | async-done | bytes 524304 | tf_op jit(solution)/shard_map/reduce_scatter | solution.py:96
  135.5 10.3 %all_gather.19 = f32[512,2,4]{0,2,1:T(4,128)S(1)} all-gather(f32[128,2,4]{0,2,1:T(4,128)S(1)} %multiply_reduce_fusion), channel_id=1, replica_groups=mesh['dp'=4,'head'=2,'srv'=4] {'dp'}, dimensions={0}, use_global_device_ids=true | all-gather | bytes 20480 | tf_op jit(solution)/shard_map/all_gather | solution.py:110
  145.8 20.5 %all-gather.6.cloned.1.call-done = bf16[512,2,512]{0,2,1:T(8,128)(2,1)} async-done(((bf16[128,2,512]{0,2,1:T(8,128)(2,1)}), bf16[512,2,512]{0,2,1:T(8,128)(2,1)}) %all-gather.6.cloned.1.call-update) | async-done | bytes 1048592 | tf_op jit(solution)/shard_map/all_gather | solution.py:33
  166.3 6.4 %fusion.1 = bf16[4,2,512,640]{2,3,1,0:T(8,128)(2,1)S(1)} fusion(f32[4,640,512,2]{2,1,3,0:T(8,128)} %get-tuple-element.88, f32[4,2,512]{2,1,0:T(2,128)S(1)} %copy.74, f32[4,2,512]{2,1,0:T(2,128)S(1)} %bitcast.134, pred[512,640]{0,1:T(8,128)(4,1)S(1)} %compare_and_fusion, bf16[512,2,4,128]{0,3,2,1:T(8,128)(2,1)} %bitcast.136, ...), kind=kOutput, calls=%fused_computation.2 | convolution fusion | flops 686817280 | bytes 17793024 | tf_op jit(solution)/shard_map/while/body/eval_jaxpr/pjgd,kgd->gjpk/dot_general | solution.py:129
  176.5 6.2 %fusion.29 = bf16[640,4,128]{2,0,1:T(8,128)(2,1)S(1)} fusion(f32[4,640,512,2]{2,1,3,0:T(8,128)} %get-tuple-element.88, f32[4,2,512]{2,1,0:T(2,128)S(1)} %bitcast.135, pred[512,640]{0,1:T(8,128)(4,1)S(1)} %compare_and_fusion, bf16[512,2,4,128]{0,3,2,1:T(8,128)(2,1)} %bitcast.137), kind=kOutput, calls=%fused_computation.28 | convolution fusion | flops 681902080 | bytes 12533760 | tf_op jit(solution)/shard_map/while/body/eval_jaxpr/gjpk,pjgd->kgd/dot_general | solution.py:123
  183.5 11.0 %all_to_all.64 = bf16[2,320,512]{2,1,0:T(8,128)(2,1)S(1)} all-to-all(bf16[2,320,512]{2,1,0:T(8,128)(2,1)S(1)} %convert_element_type.80), channel_id=1, replica_groups=mesh['dp'=4,'head'=2,'srv'=4] {'head'}, dimensions={0} | all-to-all | bytes 1310720 | tf_op jit(solution)/shard_map/all_to_all | solution.py:171
  195.6 4.0 %fusion.28 = bf16[640,4,128]{2,0,1:T(8,128)(2,1)S(1)} fusion(bf16[4,2,512,640]{2,3,1,0:T(8,128)(2,1)} %copy-done, bf16[512,2,4,128]{0,3,2,1:T(8,128)(2,1)S(1)} %bitcast.123), kind=kOutput, calls=%fused_computation.27 | convolution fusion | flops 671744000 | bytes 6946816 | tf_op jit(solution)/shard_map/while/body/eval_jaxpr/gjpk,pjgd->kgd/dot_general | solution.py:142
  200.3 10.0 %all_to_all.65 = bf16[2,320,512]{2,1,0:T(8,128)(2,1)S(1)} all-to-all(bf16[2,320,512]{2,1,0:T(8,128)(2,1)S(1)} %convert_element_type.76), channel_id=1, replica_groups=mesh['dp'=4,'head'=2,'srv'=4] {'head'}, dimensions={0} | all-to-all | bytes 1310720 | tf_op jit(solution)/shard_map/all_to_all | solution.py:164
  214.3 13.1 %reduce-scatter.14.cloned.1.call-done = bf16[80,1024]{1,0:T(8,128)(2,1)} async-done(((bf16[320,1024]{1,0:T(8,128)(2,1)}), bf16[80,1024]{1,0:T(8,128)(2,1)}) %reduce-scatter.14.cloned.1.call-update) | async-done | bytes 163856 | tf_op jit(solution)/shard_map/reduce_scatter | solution.py:183
  227.4 25.7 %reduce-scatter.12.cloned.1.call-done = bf16[80,1024]{1,0:T(8,128)(2,1)} async-done(((bf16[320,1024]{1,0:T(8,128)(2,1)}), bf16[80,1024]{1,0:T(8,128)(2,1)}) %reduce-scatter.12.cloned.1.call-update) | async-done | bytes 163856 | tf_op jit(solution)/shard_map/reduce_scatter | solution.py:180
  (58 shorter events, 19.7 us)
Async XLA Ops:
  7.2 32.5 %all-gather.4.cloned.1.call-start = ((), (), s32[]{:S(2)}) async-start(), calls=%async_computation.9 | async-start | bytes 1310720 | tf_op jit(solution)/shard_map/all_gather | solution.py:32
  11.0 17.2 %all-to-all-start = ((bf16[320,2,512]{2,0,1:T(8,128)(2,1)}), bf16[320,2,512]{2,0,1:T(8,128)(2,1)S(1)}, u32[]{:S(2)}, u32[]{:S(2)}) async-start(bf16[320,2,512]{2,0,1:T(8,128)(2,1)} %bitcast.108), calls=%async_computation | async-start | bytes 1310720 | tf_op jit(solution)/shard_map/all_to_all | solution.py:19
  28.2 10.0 %all-to-all-start.1 = ((bf16[320,2,512]{2,0,1:T(8,128)(2,1)}), bf16[320,2,512]{2,0,1:T(8,128)(2,1)S(1)}, u32[]{:S(2)}, u32[]{:S(2)}) async-start(bf16[320,2,512]{2,0,1:T(8,128)(2,1)} %bitcast.109), calls=%async_computation.1 | async-start | bytes 1310720 | tf_op jit(solution)/shard_map/all_to_all | solution.py:20
  31.7 56.3 %reduce-scatter.16.cloned.1.call-start = ((), (), s32[]{:S(2)}) async-start(), calls=%async_computation.14 | async-start | bytes 327680
  66.1 68.3 %reduce-scatter.10.cloned.1.call-start = ((), (), s32[]{:S(2)}) async-start(), calls=%async_computation.10 | async-start | bytes 2621440 | tf_op jit(solution)/shard_map/reduce_scatter | solution.py:96
  66.1 7.8 %copy-start.3 = (bf16[128,2,512]{2,1,0:T(2,128)(2,1)S(1)}, bf16[128,2,512]{2,1,0:T(2,128)(2,1)}, u32[]{:S(2)}) copy-start(bf16[128,2,512]{2,1,0:T(2,128)(2,1)} %param.8) | copy-start | bytes 786436
  73.9 92.4 %all-gather.6.cloned.1.call-start = ((), (), s32[]{:S(2)}) async-start(), calls=%async_computation.11 | async-start | bytes 1310720 | tf_op jit(solution)/shard_map/all_gather | solution.py:33
  74.9 137.4 %reduce-scatter.18.cloned.1.call-start = ((), (), s32[]{:S(2)}) async-start(), calls=%async_computation.15 | async-start | bytes 1310720
  172.7 2.4 copy-start
  176.5 19.1 %copy-start.2 = (bf16[512,2,512]{0,2,1:T(8,128)(2,1)S(1)}, bf16[512,2,512]{0,2,1:T(8,128)(2,1)}, u32[]{:S(2)}) copy-start(bf16[512,2,512]{0,2,1:T(8,128)(2,1)} %all-gather.4.cloned.1.call-done) | copy-start | bytes 3145732
  176.5 50.9 %reduce-scatter.14.cloned.1.call-start = ((), (), s32[]{:S(2)}) async-start(), calls=%async_computation.13 | async-start | bytes 819200 | tf_op jit(solution)/shard_map/reduce_scatter | solution.py:183
  182.8 28.6 %copy-start.1 = (f32[128,2,512]{0,2,1:T(8,128)S(1)}, f32[128,2,512]{0,2,1:T(8,128)}, u32[]{:S(2)}) copy-start(f32[128,2,512]{0,2,1:T(8,128)} %reduce-scatter.10.cloned.1.call-done) | copy-start | bytes 1572868
  195.5 57.6 %reduce-scatter.12.cloned.1.call-start = ((), (), s32[]{:S(2)}) async-start(), calls=%async_computation.12 | async-start | bytes 819200 | tf_op jit(solution)/shard_map/reduce_scatter | solution.py:180
Sparse Core Ops, SparseCore 0:
  10.1 29.4 all-gather.3
  66.2 21.7 reduce-scatter.15
  90.4 43.8 reduce-scatter.9
  136.3 29.9 all-gather.5
  176.6 25.3 reduce-scatter.17
  205.2 22.1 reduce-scatter.13
  230.6 22.4 reduce-scatter.11
where the time goes:
time: 263 us; the launch traced here: 260 us
  waiting for transfers between devices  114 us (43%)
  blocking collectives  62.5 us (24%)
  matrix products  31.1 us (12%)
  local copies, waits for them, and re-layouts  22.1 us (8%)
  between operations  14.4 us (5%)
  other arithmetic  8.39 us (3%)
  starting transfers between devices  7.31 us (3%)
    reduce_scatter x1, waiting for transfers between devices, local(): lax.psum_scatter(part_out, 'dp', scatter_dimension=0, tiled=True)  36.3 us
    reduce_scatter x1, waiting for transfers between devices, local(): lax.psum_scatter(spread_key.astype(jnp.bfloat16), 'srv', scatter_dimensio...  25.7 us
    all_gather x1, waiting for transfers between devices, local(): lax.all_gather(output_gradient, 'dp', axis=0, tiled=True)  20.5 us
    reduce_scatter x1, waiting for transfers between devices, local(): lax.psum_scatter(spread_value.astype(jnp.bfloat16), 'srv', scatter_dimens...  13.1 us
    unnamed x9, waiting for transfers between devices  13 us
    unnamed x20, local copies, waits for them, and re-layouts  11.7 us
    pmax x1, blocking collectives, local(): row_max = lax.pmax(local_max.reshape(query_total, pair_heads, groups), 'dp')  11.5 us
    all_to_all x1, blocking collectives, local(): lax.all_to_all(value_total.reshape(key_count, group_width).astype(jnp.bfl...  11 us
  transfers between devices with their start and end apart: 9, of which 7 were waited for; matrix products, arithmetic and copies ran while one was open for 13% of the time, Pallas kernels for 0%

commit v1 on v0

--- a/solution.py
+++ b/solution.py
@@ -1,17 +1,306 @@
+import functools
 import math
 
 import jax
 import jax.numpy as jnp
 from jax import lax
+from jax.experimental import pallas as pl
+from jax.experimental.pallas import tpu as pltpu
 from jax.sharding import PartitionSpec as P
 
 HEAD_SIZE = 128
 
 
 NEGATIVE = -1e30
-
-
-def local(queries, keys, values, output_gradient, doc_ids):
+MESH = pl.DeviceIdType.MESH
+AXES = ("dp", "head", "srv")
+
+
+def attend(sizes, qd_ref, k_ref, v_ref, doc_ref, att_ref, dq_ref, kg_ref, vg_ref,
+           qd_buf, kv_buf, kt_buf, vt_buf, docs, bias, acc, grad_out, att_out, dq_out, grad_in, total,
+           q_sem, q_got, kv_sem, kv_got, doc_sem, doc_got, att_sem, att_got, dq_sem, dq_got, g_sem, g_got):
+    dp, heads, srv, home, pair, rows, first, window = sizes
+    chunk = math.gcd(home, rows)
+    chunks = rows // chunk
+    piece = rows // srv
+    wide = pair * home
+    pad = piece
+    scale = HEAD_SIZE ** (-0.5)
+    z, x, v = (lax.axis_index(name) for name in AXES)
+    place = z * heads + x
+    base = place * rows
+    low = first + home * z
+    device_count = dp * heads * srv
+    me = place * srv + v
+
+    def device(index):
+        return (index // (heads * srv), (index // srv) % heads, index % srv)
+
+    def send(here, src, dst, send_sem, recv_sem, target):
+        @pl.when(here)
+        def _():
+            pltpu.make_async_copy(src, dst, recv_sem).start()
+
+        @pl.when(jnp.logical_not(here))
+        def _():
+            pltpu.make_async_remote_copy(
+                src_ref=src, dst_ref=dst, send_sem=send_sem, recv_sem=recv_sem,
+                device_id=target, device_id_type=MESH,
+            ).start()
+
+    def arrived(ref, sem):
+        pltpu.make_async_copy(ref, ref, sem).wait()
+
+    barrier = pltpu.get_barrier_semaphore()
+
+    def greet(index, carry):
+        @pl.when(index != me)
+        def _():
+            pl.semaphore_signal(barrier, inc=1, device_id=device(index), device_id_type=MESH)
+        return carry
+
+    lax.fori_loop(0, device_count, greet, 0)
+    pl.semaphore_wait(barrier, device_count - 1)
+
+    def key_copies(act):
+        def one(index, carry):
+            s, h = index // heads, index % heads
+            column = pl.ds(pl.multiple_of((h * srv + v) * HEAD_SIZE, HEAD_SIZE), HEAD_SIZE)
+            start = first + home * s
+            here = (s == z) & (h == x)
+            full = (base >= start) & (base + rows <= start + window)
+
+            def both(at, count, slot):
+                row = pl.multiple_of(base + at - start, chunk)
+                for which, ref in ((0, k_ref), (1, v_ref)):
+                    act(
+                        here,
+                        ref.at[pl.ds(pl.multiple_of(at, chunk), count), column],
+                        kv_buf.at[which, pl.ds(row, count), :],
+                        kv_sem.at[index, slot, which],
+                        kv_got.at[which],
+                        (s, h, v),
+                    )
+
+            @pl.when(full)
+            def _():
+                both(0, rows, 0)
+
+            def part(c, inner):
+                row = base + c * chunk
+                @pl.when(jnp.logical_not(full) & (row >= start) & (row + chunk <= start + window))
+                def _():
+                    both(c * chunk, chunk, c)
+                return inner
+
+            lax.fori_loop(0, chunks, part, 0)
+            return carry
+
+        lax.fori_loop(0, dp * heads, one, 0)
+
+    def sent(here, src, dst, send_sem, recv_sem, target):
+        @pl.when(jnp.logical_not(here))
+        def _():
+            pltpu.make_async_remote_copy(
+                src_ref=src, dst_ref=dst, send_sem=send_sem, recv_sem=recv_sem,
+                device_id=target, device_id_type=MESH,
+            ).wait_send()
+
+    def doc_copies(act):
+        for s in range(dp):
+            act(z == s, doc_ref, docs.at[z], doc_sem.at[s], doc_got.at[z], (s, x, v))
+
+    def query_copies(act):
+        for u in range(srv):
+            act(v == u, qd_ref.at[u], qd_buf.at[v], q_sem.at[u], q_got.at[v], (z, x, u))
+
+    doc_copies(send)
+    key_copies(send)
+    query_copies(send)
+
+    grad_out[:, pl.ds(0, pad), :] = jnp.zeros((2, pad, HEAD_SIZE), jnp.bfloat16)
+    grad_out[:, pl.ds(pad + window, piece), :] = jnp.zeros((2, piece, HEAD_SIZE), jnp.bfloat16)
+    acc[...] = jnp.zeros_like(acc)
+    total[...] = jnp.zeros_like(total)
+
+    for s in range(dp):
+        arrived(docs.at[s], doc_got.at[s])
+    blocks = rows * heads // 128
+    own = (low + window - home) // 128
+    query_doc = docs[own // blocks, pl.ds(own % blocks, 1), :]
+    query_at = lax.broadcasted_iota(jnp.int32, (128, home), 1) + (low + window - home)
+    for b in range(window // 128):
+        index = low // 128 + b
+        key_doc = docs[index // blocks, pl.ds(index % blocks, 1), :]
+        key_doc = jnp.broadcast_to(key_doc.astype(jnp.float32), (128, 128)).T
+        key_at = lax.broadcasted_iota(jnp.int32, (128, home), 0) + (low + b * 128)
+        same = key_doc == jnp.broadcast_to(query_doc.astype(jnp.float32), (128, home))
+        allowed = same & (key_at <= query_at)
+        tile = jnp.where(allowed, 0.0, NEGATIVE)
+        for j in range(pair):
+            bias[pl.ds(b * 128, 128), pl.ds(j * home, home)] = tile
+
+    arrived(kv_buf.at[0], kv_got.at[0])
+    arrived(kv_buf.at[1], kv_got.at[1])
+    kt_buf[...] = kv_buf[0].astype(jnp.float32).T.astype(jnp.bfloat16)
+    vt_buf[...] = kv_buf[1].astype(jnp.float32).T.astype(jnp.bfloat16)
+    for u in range(srv):
+        arrived(qd_buf.at[u], q_got.at[u])
+
+    def contract(a, b, left, right):
+        return lax.dot_general(a, b, (((left,), (right,)), ((), ())), preferred_element_type=jnp.float32)
+
+    def att_copy(act, u):
+        act(v == u, att_out.at[u], att_ref.at[v], att_sem.at[u], att_got.at[v], (z, x, u))
+
+    def dq_copy(act, u):
+        act(v == u, dq_out.at[u], dq_ref.at[v], dq_sem.at[u], dq_got.at[v], (z, x, u))
+
+    def heads_step(u, carry):
+        query = qd_buf[u, 0].reshape(wide, HEAD_SIZE)
+        grad = qd_buf[u, 1].reshape(wide, HEAD_SIZE)
+        scores = contract(kv_buf[0], query, 1, 1) + bias[...]
+        top = jnp.max(scores, axis=0, keepdims=True)
+        weights = jnp.exp2((scores - top) * (scale * math.log2(math.e)))
+        norm = jnp.sum(weights, axis=0, keepdims=True)
+        out = contract(vt_buf[...], weights.astype(jnp.bfloat16), 1, 0)
+        inverse = 1.0 / norm
+        out = (out * inverse).astype(jnp.bfloat16).astype(jnp.float32)
+        delta = jnp.sum(grad.astype(jnp.float32).T * out, axis=0, keepdims=True)
+        att_out[u] = out.T.astype(jnp.bfloat16).reshape(pair, home, HEAD_SIZE)
+        att_copy(send, u)
+        probs = weights * inverse
+        weight_grad = contract(kv_buf[1], grad, 1, 1)
+        score_grad = (probs * (weight_grad - delta)).astype(jnp.bfloat16)
+        query_grad = contract(kt_buf[...], score_grad, 1, 0) * scale
+        dq_out[u] = query_grad.T.astype(jnp.bfloat16).reshape(pair, home, HEAD_SIZE)
+        dq_copy(send, u)
+        acc[0] += contract(score_grad, query, 1, 0)
+        acc[1] += contract(probs.astype(jnp.bfloat16), grad, 1, 0)
+        return carry
+
+    lax.fori_loop(0, srv, heads_step, 0)
+    grad_out[0, pl.ds(pad, window), :] = (acc[0] * scale).astype(jnp.bfloat16)
+    grad_out[1, pl.ds(pad, window), :] = acc[1].astype(jnp.bfloat16)
+
+    lane = x * srv + v
+    pieces = window // piece + 2
+
+    def grad_copies(act):
+        def one(j, carry):
+            owner = low // piece + j
+            @pl.when(owner * piece < low + window)
+            def _():
+                at = pl.multiple_of(owner * piece - low + pad, 16)
+                act(
+                    owner == me,
+                    grad_out.at[:, pl.ds(at, piece), :],
+                    grad_in.at[z, lane],
+                    g_sem.at[j],
+                    g_got.at[z, lane],
+                    device(owner),
+                )
+            return carry
+
+        lax.fori_loop(0, pieces, one, 0)
+
+    grad_copies(send)
+
+    def gather(s, carry):
+        start = first + home * s
+        @pl.when((me * piece + piece > start) & (me * piece < start + window))
+        def _():
+            for lane_from in range(heads * srv):
+                arrived(grad_in.at[s, lane_from], g_got.at[s, lane_from])
+                total[lane_from] += grad_in[s, lane_from].astype(jnp.float32)
+        return carry
+
+    lax.fori_loop(0, dp, gather, 0)
+    for lane_from in range(heads * srv):
+        column = pl.ds(lane_from * HEAD_SIZE, HEAD_SIZE)
+        kg_ref[:, column] = total[lane_from, 0].astype(jnp.bfloat16)
+        vg_ref[:, column] = total[lane_from, 1].astype(jnp.bfloat16)
+
+    for u in range(srv):
+        arrived(att_ref.at[u], att_got.at[u])
+        arrived(dq_ref.at[u], dq_got.at[u])
+    doc_copies(sent)
+    key_copies(sent)
+    query_copies(sent)
+    for u in range(srv):
+        att_copy(sent, u)
+        dq_copy(sent, u)
+    grad_copies(sent)
+
+
+def local_window(mesh_sizes, queries, keys, values, output_gradient, doc_ids):
+    dp, heads, srv = mesh_sizes
+    home, pair, width = queries.shape
+    groups = width // HEAD_SIZE
+    rows = keys.shape[0]
+    key_total = rows * dp * heads
+    longest = key_total // 2
+    first = key_total - dp * home - longest
+    window = longest + home
+    piece = rows // srv
+    pieces = window // piece + 2
+    chunks = rows // math.gcd(home, rows)
+
+    def by_group(array):
+        return array.reshape(home, pair, groups, HEAD_SIZE).transpose(2, 1, 0, 3)
+
+    both = jnp.stack([by_group(queries), by_group(output_gradient)], axis=1)
+    docs = doc_ids.reshape(-1, 128)
+    doc_rows = -(-docs.shape[0] // 8) * 8
+    docs = jnp.pad(docs, ((0, doc_rows - docs.shape[0]), (0, 0)))
+    vmem = pl.BlockSpec(memory_space=pltpu.VMEM)
+    anywhere = pl.BlockSpec(memory_space=pl.ANY)
+    sem = pltpu.SemaphoreType.DMA
+    lanes = heads * srv
+    b16, f32 = jnp.bfloat16, jnp.float32
+    sizes = (dp, heads, srv, home, pair, rows, first, window)
+    att, dq, kg, vg = pl.pallas_call(
+        functools.partial(attend, sizes),
+        out_shape=(
+            jax.ShapeDtypeStruct((groups, pair, home, HEAD_SIZE), b16),
+            jax.ShapeDtypeStruct((groups, pair, home, HEAD_SIZE), b16),
+            jax.ShapeDtypeStruct((piece, lanes * HEAD_SIZE), b16),
+            jax.ShapeDtypeStruct((piece, lanes * HEAD_SIZE), b16),
+        ),
+        in_specs=[anywhere] * 4,
+        out_specs=(vmem, vmem, vmem, vmem),
+        scratch_shapes=[
+            pltpu.VMEM((srv, 2, pair, home, HEAD_SIZE), b16),
+            pltpu.VMEM((2, window, HEAD_SIZE), b16),
+            pltpu.VMEM((HEAD_SIZE, window), b16),
+            pltpu.VMEM((HEAD_SIZE, window), b16),
+            pltpu.VMEM((dp, doc_rows, 128), jnp.int32),
+            pltpu.VMEM((window, pair * home), f32),
+            pltpu.VMEM((2, window, HEAD_SIZE), f32),
+            pltpu.VMEM((2, window + 2 * piece, HEAD_SIZE), b16),
+            pltpu.VMEM((srv, pair, home, HEAD_SIZE), b16),
+            pltpu.VMEM((srv, pair, home, HEAD_SIZE), b16),
+            pltpu.VMEM((dp, lanes, 2, piece, HEAD_SIZE), b16),
+            pltpu.VMEM((lanes, 2, piece, HEAD_SIZE), f32),
+            sem((srv,)), sem((srv,)),
+            sem((dp * heads, chunks, 2)), sem((2,)),
+            sem((dp,)), sem((dp,)),
+            sem((srv,)), sem((srv,)),
+            sem((srv,)), sem((srv,)),
+            sem((pieces,)), sem((dp, lanes)),
+        ],
+        compiler_params=pltpu.CompilerParams(
+            collective_id=0, has_side_effects=True, vmem_limit_bytes=48 * 1024 * 1024
+        ),
+    )(both, keys, values, docs)
+
+    def by_row(array):
+        return array.transpose(2, 1, 0, 3).reshape(home, pair, width)
+
+    return by_row(att), by_row(dq), kg, vg
+
+
+def local_spread(queries, keys, values, output_gradient, doc_ids):
     home_rows, pair_heads, group_width = queries.shape
     groups = group_width // HEAD_SIZE
     scale_factor = HEAD_SIZE ** (-0.5)
@@ -195,6 +484,14 @@
         P("dp", "srv", "head"),
         P("dp"),
     )
+    sizes = tuple(mesh.shape[name] for name in AXES)
+
+    def local(queries, keys, values, output_gradient, doc_ids):
+        args = (queries, keys, values, output_gradient, doc_ids)
+        if queries.shape[2] == sizes[2] * HEAD_SIZE:
+            return local_window(sizes, *args)
+        return local_spread(*args)
+
     return jax.shard_map(
         local,
         mesh=mesh,

time: 263 us -> 77.5 us (0.29)
  the two profiles are of different devices: /device:TPU:13 before, /device:TPU:29 now
where the time goes in v1:
time: 77.5 us; the launch traced here: 77.3 us
  Pallas kernels  68.8 us (89%)
  local copies, waits for them, and re-layouts  7.72 us (10%)
    pallas_call x1, Pallas kernels, local_window(): pl.pallas_call(functools.partial(attend, sizes), out_shape=(jax.ShapeDtyp...  68.8 us
    unnamed x12, local copies, waits for them, and re-layouts  6.32 us

profile of v1, /device:TPU:29, one launch (start us, length us, event | category | flops | bytes accessed | tf_op | source)
XLA Modules:
  0.0 77.3 jit_solution(15227045358959521895)
XLA Ops:
  0.6 0.7 pad.4.doc_ref
  1.3 1.1 %copy.9 = bf16[128,2,512]{0,2,1:T(8,128)(2,1)S(1)} copy(bf16[128,2,512]{2,1,0:T(2,128)(2,1)} %param.5) | data formatting | bytes 524288 | tf_op args[0]
  2.5 0.0 copy-start.2
  2.5 0.2 copy.10
  2.7 0.8 copy-done.2
  3.4 0.2 copy.11
  3.7 0.0 copy-start.1
  3.7 0.2 copy.12
  3.9 0.0 copy-start
  3.9 0.1 pad_maximum_fusion.qd_ref
  3.9 0.8 %copy-done.1 = bf16[320,1024]{1,0:T(8,128)(2,1)S(1)} copy-done((bf16[320,1024]{1,0:T(8,128)(2,1)S(1)}, bf16[320,1024]{1,0:T(8,128)(2,1)}, u32[]{:S(2)}) %copy-start.1) | copy-done | bytes 655384
  4.8 0.2 copy-done
  5.0 68.8 %shard_map.84 = (bf16[4,2,128,128]{3,2,1,0:T(8,128)(2,1)S(1)}, bf16[4,2,128,128]{3,2,1,0:T(8,128)(2,1)S(1)}, bf16[80,1024]{1,0:T(8,128)(2,1)S(1)}, bf16[80,1024]{1,0:T(8,128)(2,1)S(1)}) custom-call(bf16[4,2,2,128,128]{4,3,2,1,0:T(8,128)(2,1)S(1)} %pad_maximum_fusion.qd_ref, bf16[320,1024]{1,0:T(8,128)(2,1)S(1)} %copy-done, bf16[320,1024]{1,0:T(8,128)(2,1)S(1)} %copy-done.1, ...), custom_call_target="tpu_custom_call" | custom-call | tf_op jit(solution)/shard_map/pallas_call | solution.py:262
  73.8 0.2 copy.13
  74.0 0.9 %copy.15 = bf16[128,2,512]{2,1,0:T(2,128)(2,1)} copy(bf16[128,2,512]{0,2,1:T(8,128)(2,1)S(1)} %bitcast.15) | data formatting | bytes 524288
  74.9 0.2 copy.14
  75.1 0.9 %copy.16 = bf16[128,2,512]{2,1,0:T(2,128)(2,1)} copy(bf16[128,2,512]{0,2,1:T(8,128)(2,1)S(1)} %bitcast.16) | data formatting | bytes 524288
  76.0 0.7 copy.19
  76.6 0.7 copy.20
Async XLA Ops:
  2.5 1.0 %copy-start.2 = (bf16[128,2,512]{2,1,0:T(2,128)(2,1)S(1)}, bf16[128,2,512]{2,1,0:T(2,128)(2,1)}, u32[]{:S(2)}) copy-start(bf16[128,2,512]{2,1,0:T(2,128)(2,1)} %param.8) | copy-start | bytes 786436
  3.7 1.1 %copy-start.1 = (bf16[320,1024]{1,0:T(8,128)(2,1)S(1)}, bf16[320,1024]{1,0:T(8,128)(2,1)}, u32[]{:S(2)}) copy-start(bf16[320,1024]{1,0:T(8,128)(2,1)} %v_ref.1) | copy-start | bytes 1966084
  3.9 1.1 %copy-start = (bf16[320,1024]{1,0:T(8,128)(2,1)S(1)}, bf16[320,1024]{1,0:T(8,128)(2,1)}, u32[]{:S(2)}) copy-start(bf16[320,1024]{1,0:T(8,128)(2,1)} %k_ref.1) | copy-start | bytes 1966084

commit v2 on v0

--- a/solution.py
+++ b/solution.py
@@ -1,17 +1,393 @@
+import functools
 import math
 
 import jax
 import jax.numpy as jnp
 from jax import lax
+from jax.experimental import pallas as pl
+from jax.experimental.pallas import tpu as pltpu
 from jax.sharding import PartitionSpec as P
 
 HEAD_SIZE = 128
 
 
 NEGATIVE = -1e30
-
-
-def local(queries, keys, values, output_gradient, doc_ids):
+MESH = pl.DeviceIdType.MESH
+AXES = ("dp", "head", "srv")
+
+
+TILE = 128
+
+
+def attend(sizes, qd_ref, k_ref, v_ref, doc_ref, att_ref, dq_ref, g_ref,
+           qd_buf, kv_buf, docs, scores, top, norm, out_t, dq_t, acc, part, up_in, down_in, owned, att_out, dq_out,
+           q_sem, q_got, kv_sem, kv_got, relay_sem, doc_sem, doc_got, att_sem, att_got, dq_sem, dq_got,
+           part_sem, up_got, down_got, g_sem, g_got):
+    dp, heads, srv, home, pair, rows, first, window = sizes
+    chunk = math.gcd(TILE, rows)
+    chunks = rows // chunk
+    piece = rows // srv
+    wide = pair * home
+    every = srv * wide
+    tiles = window // TILE
+    blocks = rows * heads // TILE
+    lanes = heads * srv
+    scale = HEAD_SIZE ** (-0.5)
+    exponent = scale * math.log2(math.e)
+    z, x, v = (lax.axis_index(name) for name in AXES)
+    base = (z * heads + x) * rows
+    low = first + home * z
+    low_tile = low // TILE
+    own_first = jnp.maximum(z * blocks - low_tile, 0)
+    lane = x * srv + v
+
+    def copy(src, dst, send_sem, recv_sem, target):
+        return pltpu.make_async_remote_copy(
+            src_ref=src, dst_ref=dst, send_sem=send_sem, recv_sem=recv_sem,
+            device_id=target, device_id_type=MESH,
+        )
+
+    def send(here, src, dst, send_sem, recv_sem, target):
+        @pl.when(here)
+        def _():
+            pltpu.make_async_copy(src, dst, recv_sem).start()
+
+        @pl.when(jnp.logical_not(here))
+        def _():
+            copy(src, dst, send_sem, recv_sem, target).start()
+
+    def sent(here, src, dst, send_sem, recv_sem, target):
+        @pl.when(jnp.logical_not(here))
+        def _():
+            copy(src, dst, send_sem, recv_sem, target).wait_send()
+
+    def arrived(ref, sem):
+        pltpu.make_async_copy(ref, ref, sem).wait()
+
+    barrier = pltpu.get_barrier_semaphore()
+
+    def greet(index, carry):
+        s, h, u = index // lanes, (index // srv) % heads, index % srv
+        beside = (s - z == 1) | (z - s == 1)
+        partner = (s == z) | ((u == v) & (beside | (h == x)))
+        myself = (s == z) & (h == x) & (u == v)
+
+        @pl.when(partner & jnp.logical_not(myself))
+        def _():
+            pl.semaphore_signal(barrier, inc=1, device_id=(s, h, u), device_id_type=MESH)
+        return carry
+
+    lax.fori_loop(0, dp * lanes, greet, 0)
+    sides = jnp.where(z > 0, 1, 0) + jnp.where(z < dp - 1, 1, 0)
+    pl.semaphore_wait(barrier, lanes - 1 + sides * heads + dp - 1 - sides)
+
+    def key_copies(act):
+        def one(index, carry):
+            side, h = index // heads, index % heads
+            s = z + jnp.where(side == 0, -1, jnp.where(side == 1, 1, 0))
+            column = pl.ds(pl.multiple_of((h * srv + v) * HEAD_SIZE, HEAD_SIZE), HEAD_SIZE)
+            start = first + home * s
+
+            def each(c, inner):
+                row = base + c * chunk - start
+
+                @pl.when((s >= 0) & (s < dp) & (row >= 0) & (row < window))
+                def _():
+                    for which, ref in ((0, k_ref), (1, v_ref)):
+                        act(
+                            (s == z) & (h == x),
+                            ref.at[pl.ds(pl.multiple_of(c * chunk, chunk), chunk), column],
+                            kv_buf.at[row // TILE, which, pl.ds(pl.multiple_of(row % TILE, chunk), chunk), :],
+                            kv_sem.at[index, c, which],
+                            kv_got.at[row // TILE],
+                            (s, h, v),
+                        )
+                return inner
+
+            lax.fori_loop(0, chunks, each, 0)
+            return carry
+
+        lax.fori_loop(0, 3 * heads, one, 0)
+
+    def doc_copies(act):
+        for s in range(dp):
+            act(z == s, doc_ref, docs.at[z], doc_sem.at[s], doc_got.at[z], (s, x, v))
+
+    def query_copies(act):
+        for u in range(srv):
+            act(v == u, qd_ref.at[u], qd_buf.at[:, v], q_sem.at[u], q_got.at[v], (z, x, u))
+
+    doc_copies(send)
+    query_copies(send)
+    key_copies(send)
+
+    top[...] = jnp.full_like(top, NEGATIVE / 10)
+    norm[...] = jnp.zeros_like(norm)
+    out_t[...] = jnp.zeros_like(out_t)
+    dq_t[...] = jnp.zeros_like(dq_t)
+    owned[...] = jnp.zeros_like(owned)
+
+    def contract(a, b, left, right):
+        return lax.dot_general(a, b, (((left,), (right,)), ((), ())), preferred_element_type=jnp.float32)
+
+    def turned(a):
+        return a.astype(jnp.float32).T.astype(jnp.bfloat16)
+
+    for s in range(dp):
+        arrived(docs.at[s], doc_got.at[s])
+    home_tile = low_tile + tiles - 1
+    query_doc = docs[home_tile // blocks, pl.ds(home_tile % blocks, 1), :]
+    query_doc = jnp.broadcast_to(query_doc.astype(jnp.float32), (TILE, home))
+    query_at = lax.broadcasted_iota(jnp.int32, (TILE, home), 1) + home_tile * TILE
+    for u in range(srv):
+        arrived(qd_buf.at[:, u], q_got.at[u])
+
+    def relays(act, tile):
+        shard = (low_tile + tile) // blocks
+
+        @pl.when((shard > z) & (z > 0) & (tile < tiles - 1))
+        def _():
+            act(copy(kv_buf.at[tile], kv_buf.at[tile + 1], relay_sem.at[tile], kv_got.at[tile + 1], (z - 1, x, v)))
+
+        @pl.when((shard < z) & (z < dp - 1) & (tile > 0))
+        def _():
+            act(copy(kv_buf.at[tile], kv_buf.at[tile - 1], relay_sem.at[tile], kv_got.at[tile - 1], (z + 1, x, v)))
+
+    def forward(i, carry):
+        tile = jnp.where(i < tiles - own_first, own_first + i, tiles - 1 - i)
+        index = low_tile + tile
+        arrived(kv_buf.at[tile], kv_got.at[tile])
+        relays(lambda c: c.start(), tile)
+        key_doc = docs[index // blocks, pl.ds(index % blocks, 1), :]
+        key_doc = jnp.broadcast_to(key_doc.astype(jnp.float32), (TILE, TILE)).T
+        key_at = lax.broadcasted_iota(jnp.int32, (TILE, home), 0) + index * TILE
+        bias = jnp.where((key_doc == query_doc) & (key_at <= query_at), 0.0, NEGATIVE)
+        value_t = turned(kv_buf[tile, 1])
+        keys = kv_buf[tile, 0]
+        for u in range(srv):
+            at = pl.ds(u * wide, wide)
+            raw = contract(keys, qd_buf[0, u], 1, 1) + jnp.concatenate([bias] * pair, axis=1)
+            scores[tile, :, at] = raw
+            old = top[:, at]
+            new = jnp.maximum(old, jnp.max(raw, axis=0, keepdims=True))
+            weights = jnp.exp2((raw - new) * exponent)
+            shrink = jnp.exp2((old - new) * exponent)
+            top[:, at] = new
+            norm[:, at] = norm[:, at] * shrink + jnp.sum(weights, axis=0, keepdims=True)
+            out_t[:, at] = out_t[:, at] * shrink + contract(value_t, weights.astype(jnp.bfloat16), 1, 0)
+        return carry
+
+    lax.fori_loop(0, tiles, forward, 0)
+
+    def att_copy(act, u):
+        act(v == u, att_out.at[u], att_ref.at[v], att_sem.at[u], att_got.at[v], (z, x, u))
+
+    def dq_copy(act, u):
+        act(v == u, dq_out.at[u], dq_ref.at[v], dq_sem.at[u], dq_got.at[v], (z, x, u))
+
+    for u in range(srv):
+        at = pl.ds(u * wide, wide)
+        out = (out_t[:, at] / norm[:, at]).T.astype(jnp.bfloat16)
+        att_out[u] = out
+        att_copy(send, u)
+        product = qd_buf[1, u].astype(jnp.float32) * out.astype(jnp.float32)
+        out_t[pl.ds(0, 1), at] = jnp.sum(product.T, axis=0, keepdims=True)
+        top[:, at] = top[:, at] * exponent + jnp.log2(norm[:, at])
+
+    def part_copies(act, tile):
+        shard = (low_tile + tile) // blocks
+
+        @pl.when(shard > z)
+        def _():
+            act(copy(part.at[tile], up_in.at[tile], part_sem.at[tile], up_got.at[tile], (z + 1, x, v)))
+
+        @pl.when(shard < z)
+        def _():
+            act(copy(part.at[tile], down_in.at[tile], part_sem.at[tile], down_got.at[tile], (z - 1, x, v)))
+
+    def backward(i, carry):
+        tile = jnp.where(i == 0, tiles - 1, jnp.where(i <= own_first, i - 1, tiles - 1 + own_first - i))
+        index = low_tile + tile
+        shard = index // blocks
+        key_t = turned(kv_buf[tile, 0])
+        values = kv_buf[tile, 1]
+        key_grad = jnp.zeros((TILE, HEAD_SIZE), jnp.float32)
+        value_grad = jnp.zeros((TILE, HEAD_SIZE), jnp.float32)
+        for u in range(srv):
+            at = pl.ds(u * wide, wide)
+            probs = jnp.exp2(scores[tile, :, at] * exponent - top[:, at])
+            weight_grad = contract(values, qd_buf[1, u], 1, 1)
+            score_grad = (probs * (weight_grad - out_t[pl.ds(0, 1), at])).astype(jnp.bfloat16)
+            key_grad = key_grad + contract(score_grad, qd_buf[0, u], 1, 0)
+            value_grad = value_grad + contract(probs.astype(jnp.bfloat16), qd_buf[1, u], 1, 0)
+            dq_t[:, at] += contract(key_t, score_grad, 1, 0)
+        acc[0] = key_grad * scale
+        acc[1] = value_grad
+
+        @pl.when((shard >= z) & (z > 0) & (tile < tiles - 1))
+        def _():
+            arrived(up_in.at[tile + 1], up_got.at[tile + 1])
+            acc[...] += up_in[tile + 1].astype(jnp.float32)
+
+        @pl.when((shard <= z) & (z < dp - 1) & (tile > 0))
+        def _():
+            arrived(down_in.at[tile - 1], down_got.at[tile - 1])
+            acc[...] += down_in[tile - 1].astype(jnp.float32)
+
+        @pl.when(shard == z)
+        def _():
+            owned[:, pl.ds(pl.multiple_of((index - z * blocks) * TILE, TILE), TILE), :] = acc[...].astype(jnp.bfloat16)
+
+        @pl.when(shard != z)
+        def _():
+            part[tile] = acc[...].astype(jnp.bfloat16)
+        part_copies(lambda c: c.start(), tile)
+        return carry
+
+    lax.fori_loop(0, tiles, backward, 0)
+
+    @pl.when((z > 0) & ((low_tile - 1) // blocks == z))
+    def _():
+        arrived(up_in.at[0], up_got.at[0])
+        owned[:, pl.ds(pl.multiple_of((low_tile - 1 - z * blocks) * TILE, TILE), TILE), :] = up_in[0]
+
+    def grad_copies(act):
+        column = pl.ds(pl.multiple_of(lane * HEAD_SIZE, HEAD_SIZE), HEAD_SIZE)
+        for j in range(lanes):
+            act(
+                lane == j,
+                owned.at[:, pl.ds(j * piece, piece), :],
+                g_ref.at[:, :, column],
+                g_sem.at[j],
+                g_got.at[lane],
+                (z, j // srv, j % srv),
+            )
+
+    grad_copies(send)
+    for u in range(srv):
+        dq_out[u] = (dq_t[:, pl.ds(u * wide, wide)] * scale).T.astype(jnp.bfloat16)
+        dq_copy(send, u)
+
+    doc_copies(sent)
+    key_copies(sent)
+    query_copies(sent)
+
+    def settle(tile, carry):
+        relays(lambda c: c.wait_send(), tile)
+        part_copies(lambda c: c.wait_send(), tile)
+        return carry
+
+    lax.fori_loop(0, tiles, settle, 0)
+    for u in range(srv):
+        att_copy(sent, u)
+        arrived(att_ref.at[u], att_got.at[u])
+    for u in range(srv):
+        dq_copy(sent, u)
+        arrived(dq_ref.at[u], dq_got.at[u])
+    grad_copies(sent)
+    for j in range(lanes):
+        arrived(g_ref.at[:, :, pl.ds(j * HEAD_SIZE, HEAD_SIZE)], g_got.at[j])
+
+
+def window_sizes(mesh_sizes, queries, keys):
+    dp, heads, srv = mesh_sizes
+    home, pair, width = queries.shape
+    rows = keys.shape[0]
+    key_total = rows * dp * heads
+    longest = key_total // 2
+    first = key_total - dp * home - longest
+    return (dp, heads, srv, home, pair, rows, first, longest + home)
+
+
+def window_fits(sizes, width):
+    dp, heads, srv, home, pair, rows, first, window = sizes
+    shard = rows * heads
+    if width != srv * HEAD_SIZE or home != TILE or shard % TILE or first < 0 or first % TILE or window % TILE:
+        return False
+    if rows % srv or (rows // srv) % 16 or rows % 16:
+        return False
+    blocks, tiles, start = shard // TILE, window // TILE, first // TILE
+    for s in range(dp):
+        held = set(range(start + s, start + s + tiles))
+        for other in (s - 1, s + 1):
+            if 0 <= other < dp:
+                for tile in range(start + other, start + other + tiles):
+                    beyond = tile // blocks > s if other < s else tile // blocks < s
+                    owned = tile // blocks == s
+                    if (beyond or owned) and tile not in held and not (owned and other < s and tile == start + other):
+                        return False
+                    through = tile // blocks > s if other < s else tile // blocks < s
+                    if through and tile not in held:
+                        return False
+    return True
+
+
+def local_window(sizes, queries, keys, values, output_gradient, doc_ids):
+    dp, heads, srv, home, pair, rows, first, window = sizes
+    width = queries.shape[2]
+    groups = width // HEAD_SIZE
+    wide = pair * home
+    tiles = window // TILE
+    piece = rows // srv
+    chunks = rows // math.gcd(TILE, rows)
+
+    def by_group(array):
+        return array.reshape(home, pair, groups, HEAD_SIZE).transpose(2, 1, 0, 3).reshape(groups, wide, HEAD_SIZE)
+
+    both = jnp.stack([by_group(queries), by_group(output_gradient)], axis=1)
+    docs = doc_ids.reshape(-1, TILE)
+    doc_rows = -(-docs.shape[0] // 8) * 8
+    docs = jnp.pad(docs, ((0, doc_rows - docs.shape[0]), (0, 0)))
+    vmem = pl.BlockSpec(memory_space=pltpu.VMEM)
+    anywhere = pl.BlockSpec(memory_space=pl.ANY)
+    sem = pltpu.SemaphoreType.DMA
+    lanes = heads * srv
+    b16, f32 = jnp.bfloat16, jnp.float32
+    att, dq, kv = pl.pallas_call(
+        functools.partial(attend, sizes),
+        out_shape=(
+            jax.ShapeDtypeStruct((groups, wide, HEAD_SIZE), b16),
+            jax.ShapeDtypeStruct((groups, wide, HEAD_SIZE), b16),
+            jax.ShapeDtypeStruct((2, piece, lanes * HEAD_SIZE), b16),
+        ),
+        in_specs=[anywhere] * 4,
+        out_specs=(vmem, vmem, vmem),
+        scratch_shapes=[
+            pltpu.VMEM((2, srv, wide, HEAD_SIZE), b16),
+            pltpu.VMEM((tiles, 2, TILE, HEAD_SIZE), b16),
+            pltpu.VMEM((dp, doc_rows, TILE), jnp.int32),
+            pltpu.VMEM((tiles, TILE, srv * wide), f32),
+            pltpu.VMEM((1, srv * wide), f32),
+            pltpu.VMEM((1, srv * wide), f32),
+            pltpu.VMEM((HEAD_SIZE, srv * wide), f32),
+            pltpu.VMEM((HEAD_SIZE, srv * wide), f32),
+            pltpu.VMEM((2, TILE, HEAD_SIZE), f32),
+            pltpu.VMEM((tiles, 2, TILE, HEAD_SIZE), b16),
+            pltpu.VMEM((tiles, 2, TILE, HEAD_SIZE), b16),
+            pltpu.VMEM((tiles, 2, TILE, HEAD_SIZE), b16),
+            pltpu.VMEM((2, rows * heads, HEAD_SIZE), b16),
+            pltpu.VMEM((srv, wide, HEAD_SIZE), b16),
+            pltpu.VMEM((srv, wide, HEAD_SIZE), b16),
+            sem((srv,)), sem((srv,)),
+            sem((3 * heads, chunks, 2)), sem((tiles,)), sem((tiles,)),
+            sem((dp,)), sem((dp,)),
+            sem((srv,)), sem((srv,)),
+            sem((srv,)), sem((srv,)),
+            sem((tiles,)), sem((tiles,)), sem((tiles,)),
+            sem((lanes,)), sem((lanes,)),
+        ],
+        compiler_params=pltpu.CompilerParams(
+            collective_id=0, has_side_effects=True, vmem_limit_bytes=40 * 1024 * 1024
+        ),
+    )(both, keys, values, docs)
+
+    def by_row(array):
+        return array.reshape(groups, pair, home, HEAD_SIZE).transpose(2, 1, 0, 3).reshape(home, pair, width)
+
+    return by_row(att), by_row(dq), kv[0], kv[1]
+
+
+def local_spread(queries, keys, values, output_gradient, doc_ids):
     home_rows, pair_heads, group_width = queries.shape
     groups = group_width // HEAD_SIZE
     scale_factor = HEAD_SIZE ** (-0.5)
@@ -195,6 +571,15 @@
         P("dp", "srv", "head"),
         P("dp"),
     )
+    mesh_sizes = tuple(mesh.shape[name] for name in AXES)
+
+    def local(queries, keys, values, output_gradient, doc_ids):
+        args = (queries, keys, values, output_gradient, doc_ids)
+        sizes = window_sizes(mesh_sizes, queries, keys)
+        if window_fits(sizes, queries.shape[2]):
+            return local_window(sizes, *args)
+        return local_spread(*args)
+
     return jax.shard_map(
         local,
         mesh=mesh,

time: 263 us -> 59.7 us (0.23)
  waiting for transfers between devices: 114 us -> 0 us
  blocking collectives: 62.5 us -> 0 us
  Pallas kernels: 0 us -> 51.2 us
  matrix products: 31.1 us -> 0 us
  local copies, waits for them, and re-layouts: 22.1 us -> 6.89 us
  between operations: 14.4 us -> 0.7 us
  other arithmetic: 8.39 us -> 0.05 us
  starting transfers between devices: 7.31 us -> 0 us
    reduce_scatter x3 -> x0, waiting for transfers between devices: 75.1 us -> none  [the longest x1 36.3 us: local(): lax.psum_scatter(part_out, 'dp', scatter_dimension=0, tiled=True)]
    pallas_call x0 -> x1, Pallas kernels: none -> 51.2 us  [local_window(): pl.pallas_call(functools.partial(attend, sizes), out_shape=(jax.ShapeDtyp...]
    dot_general x6 -> x0, matrix products: 31.1 us -> none  [the longest x1 7.18 us: scores_of(): jnp.einsum('pjgd,kgd->gjpk', query_block, key_heads, preferred_element_ty...]
    all_gather x3 -> x0, blocking collectives: 29.9 us -> none  [the longest x1 10.9 us: local(): all_docs = lax.all_gather(doc_ids, 'dp', axis=0, tiled=True)]
    all_gather x2 -> x0, waiting for transfers between devices: 21.8 us -> none  [the longest x1 20.5 us: local(): lax.all_gather(output_gradient, 'dp', axis=0, tiled=True)]
    all_to_all x2 -> x0, blocking collectives: 21 us -> none  [the longest x1 11 us: local(): lax.all_to_all(value_total.reshape(key_count, group_width).astype(jnp.bfl...]
    unnamed x9 -> x0, waiting for transfers between devices: 13 us -> none
    pmax x1 -> x0, blocking collectives: 11.5 us -> none  [local(): row_max = lax.pmax(local_max.reshape(query_total, pair_heads, groups), 'dp')]
  transfers between devices with their start and end apart: 9 -> 0, of which waited for: 7 -> 0; matrix products, arithmetic and copies ran while one was open for 13% -> 0% of each run, Pallas kernels for 0% -> 0%
where the time goes in v2:
time: 59.7 us; the launch traced here: 58.9 us
  Pallas kernels  51.2 us (86%)
  local copies, waits for them, and re-layouts  6.89 us (12%)
  between operations  0.7 us (1%)
    pallas_call x1, Pallas kernels, local_window(): pl.pallas_call(functools.partial(attend, sizes), out_shape=(jax.ShapeDtyp...  51.2 us
    unnamed x6, local copies, waits for them, and re-layouts  2.08 us
    reshape x2, local copies, waits for them, and re-layouts, by_row(): array.reshape(groups, pair, home, HEAD_SIZE).transpose(2, 1, 0, 3)  1.61 us
    reshape x4, local copies, waits for them, and re-layouts, by_group(): array.reshape(home, pair, groups, HEAD_SIZE).transpose(2, 1, 0, 3)  1.36 us

profile of v2, /device:TPU:13, one launch (start us, length us, event | category | flops | bytes accessed | tf_op | source)
XLA Modules:
  0.0 58.9 jit_solution(14173209940070485315)
XLA Ops:
  0.6 0.7 %pad.4.doc_ref = s32[8,128]{1,0:T(8,128)S(1)} pad(s32[5,128]{1,0:T(8,128)} %bitcast.21, s32[]{:T(128)} %constant.0.clone.1), padding=0_3x0_0 | pad | bytes 6660 | tf_op jit(solution)/shard_map/jit(_pad)/pad | solution.py:340
  1.3 1.1 %reshape.29 = bf16[128,2,4,128]{3,2,1,0:T(4,128)(2,1)S(1)} reshape(bf16[128,2,512]{2,1,0:T(2,128)(2,1)} %param.5) | data formatting | bytes 524288 | tf_op jit(solution)/shard_map/reshape | solution.py:335
  2.4 0.0 copy-start.2
  2.5 0.9 %copy-done.2 = bf16[128,2,512]{2,1,0:T(2,128)(2,1)S(1)} copy-done((bf16[128,2,512]{2,1,0:T(2,128)(2,1)S(1)}, bf16[128,2,512]{2,1,0:T(2,128)(2,1)}, u32[]{:S(2)}) %copy-start.2) | copy-done | bytes 262168
  3.4 0.2 reshape.30
  3.6 0.0 copy-start.1
  3.6 0.0 copy-start
  3.6 0.1 pad_maximum_fusion.qd_ref
  3.7 1.0 %copy-done.1 = bf16[320,1024]{1,0:T(8,128)(2,1)S(1)} copy-done((bf16[320,1024]{1,0:T(8,128)(2,1)S(1)}, bf16[320,1024]{1,0:T(8,128)(2,1)}, u32[]{:S(2)}) %copy-start.1) | copy-done | bytes 655384
  4.7 0.2 copy-done
  4.9 51.2 %shard_map.84 = (bf16[4,256,128]{2,1,0:T(8,128)(2,1)S(1)}, bf16[4,256,128]{2,1,0:T(8,128)(2,1)S(1)}, bf16[2,80,1024]{2,1,0:T(8,128)(2,1)S(1)}) custom-call(bf16[4,2,256,128]{3,2,1,0:T(8,128)(2,1)S(1)} %pad_maximum_fusion.qd_ref, bf16[320,1024]{1,0:T(8,128)(2,1)S(1)} %copy-done, bf16[320,1024]{1,0:T(8,128)(2,1)S(1)} %copy-done.1, s32[8,128]{1,0:T(8,128)S(1)} %pad.4.doc_ref), custom_call_target="tpu_custom_call" | custom-call | tf_op jit(solution)/shard_map/pallas_call | solution.py:346
  56.1 0.2 copy.11
  56.3 0.8 %reshape.33 = bf16[128,2,512]{2,1,0:T(2,128)(2,1)} reshape(bf16[128,2,4,128]{3,2,1,0:T(4,128)(2,1)S(1)} %copy.11) | data formatting | bytes 524288 | tf_op jit(solution)/shard_map/reshape | solution.py:385
  57.1 0.2 copy.12
  57.3 0.8 %reshape.35 = bf16[128,2,512]{2,1,0:T(2,128)(2,1)} reshape(bf16[128,2,4,128]{3,2,1,0:T(4,128)(2,1)S(1)} %copy.12) | data formatting | bytes 524288 | tf_op jit(solution)/shard_map/reshape | solution.py:385
  58.1 0.7 %slice_bitcast_fusion = (bf16[80,1024]{1,0:T(8,128)(2,1)}, bf16[80,1024]{1,0:T(8,128)(2,1)}) fusion(bf16[2,80,1024]{2,1,0:T(8,128)(2,1)S(1)} %get-tuple-element.9), kind=kLoop, calls=%fused_computation.1 | loop fusion | bytes 655360 | tf_op jit(solution)/shard_map/squeeze | solution.py:387
  (2 shorter events, 0.1 us)
Async XLA Ops:
  2.4 1.0 %copy-start.2 = (bf16[128,2,512]{2,1,0:T(2,128)(2,1)S(1)}, bf16[128,2,512]{2,1,0:T(2,128)(2,1)}, u32[]{:S(2)}) copy-start(bf16[128,2,512]{2,1,0:T(2,128)(2,1)} %param.8) | copy-start | bytes 786436
  3.6 1.1 %copy-start.1 = (bf16[320,1024]{1,0:T(8,128)(2,1)S(1)}, bf16[320,1024]{1,0:T(8,128)(2,1)}, u32[]{:S(2)}) copy-start(bf16[320,1024]{1,0:T(8,128)(2,1)} %v_ref.1) | copy-start | bytes 1966084
  3.6 1.2 %copy-start = (bf16[320,1024]{1,0:T(8,128)(2,1)S(1)}, bf16[320,1024]{1,0:T(8,128)(2,1)}, u32[]{:S(2)}) copy-start(bf16[320,1024]{1,0:T(8,128)(2,1)} %k_ref.1) | copy-start | bytes 1966084

commit v3 on v2

--- a/solution.py
+++ b/solution.py
@@ -17,10 +17,11 @@
 
 
 TILE = 128
+LAG = 3
 
 
 def attend(sizes, qd_ref, k_ref, v_ref, doc_ref, att_ref, dq_ref, g_ref,
-           qd_buf, kv_buf, docs, scores, top, norm, out_t, dq_t, acc, part, up_in, down_in, owned, att_out, dq_out,
+           qd_buf, kv_buf, docs, scores, top, norm, delta, out_t, grad_t, dq_t, acc, part, up_in, down_in, owned, att_out, dq_out,
            q_sem, q_got, kv_sem, kv_got, relay_sem, doc_sem, doc_got, att_sem, att_got, dq_sem, dq_got,
            part_sem, up_got, down_got, g_sem, g_got):
     dp, heads, srv, home, pair, rows, first, window = sizes
@@ -141,6 +142,7 @@
     query_at = lax.broadcasted_iota(jnp.int32, (TILE, home), 1) + home_tile * TILE
     for u in range(srv):
         arrived(qd_buf.at[:, u], q_got.at[u])
+        grad_t[:, pl.ds(u * wide, wide)] = qd_buf[1, u].astype(jnp.float32).T
 
     def relays(act, tile):
         shard = (low_tile + tile) // blocks
@@ -187,11 +189,9 @@
 
     for u in range(srv):
         at = pl.ds(u * wide, wide)
-        out = (out_t[:, at] / norm[:, at]).T.astype(jnp.bfloat16)
-        att_out[u] = out
-        att_copy(send, u)
-        product = qd_buf[1, u].astype(jnp.float32) * out.astype(jnp.float32)
-        out_t[pl.ds(0, 1), at] = jnp.sum(product.T, axis=0, keepdims=True)
+        out = (out_t[:, at] / norm[:, at]).astype(jnp.bfloat16).astype(jnp.float32)
+        out_t[:, at] = out
+        delta[:, at] = jnp.sum(grad_t[:, at] * out, axis=0, keepdims=True)
         top[:, at] = top[:, at] * exponent + jnp.log2(norm[:, at])
 
     def part_copies(act, tile):
@@ -205,10 +205,49 @@
         def _():
             act(copy(part.at[tile], down_in.at[tile], part_sem.at[tile], down_got.at[tile], (z - 1, x, v)))
 
-    def backward(i, carry):
-        tile = jnp.where(i == 0, tiles - 1, jnp.where(i <= own_first, i - 1, tiles - 1 + own_first - i))
+    def grad_copies(act, least, most):
+        column = pl.ds(pl.multiple_of(lane * HEAD_SIZE, HEAD_SIZE), HEAD_SIZE)
+
+        def one(j, carry):
+            @pl.when((j * piece >= least) & (j * piece < most))
+            def _():
+                act(
+                    lane == j,
+                    owned.at[:, pl.ds(pl.multiple_of(j * piece, 16), piece), :],
+                    g_ref.at[:, :, column],
+                    g_sem.at[j],
+                    g_got.at[lane],
+                    (z, j // srv, j % srv),
+                )
+            return carry
+
+        lax.fori_loop(0, lanes, one, 0)
+
+    def place(i):
+        return jnp.where(i == 0, tiles - 1, jnp.where(i <= own_first, i - 1, tiles - 1 + own_first - i))
+
+    def waits_for(tile):
+        shard = (low_tile + tile) // blocks
+        above = (shard >= z) & (z > 0) & (tile < tiles - 1)
+        below = (shard <= z) & (z < dp - 1) & (tile > 0)
+        return above, below
+
+    def finish(tile):
         index = low_tile + tile
         shard = index // blocks
+
+        @pl.when(shard == z)
+        def _():
+            row = (index - z * blocks) * TILE
+            owned[:, pl.ds(pl.multiple_of(row, TILE), TILE), :] = acc[tile].astype(jnp.bfloat16)
+            grad_copies(send, row, row + TILE)
+
+        @pl.when(shard != z)
+        def _():
+            part[tile] = acc[tile].astype(jnp.bfloat16)
+        part_copies(lambda c: c.start(), tile)
+
+    def compute(tile):
         key_t = turned(kv_buf[tile, 0])
         values = kv_buf[tile, 1]
         key_grad = jnp.zeros((TILE, HEAD_SIZE), jnp.float32)
@@ -217,56 +256,67 @@
             at = pl.ds(u * wide, wide)
             probs = jnp.exp2(scores[tile, :, at] * exponent - top[:, at])
             weight_grad = contract(values, qd_buf[1, u], 1, 1)
-            score_grad = (probs * (weight_grad - out_t[pl.ds(0, 1), at])).astype(jnp.bfloat16)
+            score_grad = (probs * (weight_grad - delta[:, at])).astype(jnp.bfloat16)
             key_grad = key_grad + contract(score_grad, qd_buf[0, u], 1, 0)
             value_grad = value_grad + contract(probs.astype(jnp.bfloat16), qd_buf[1, u], 1, 0)
             dq_t[:, at] += contract(key_t, score_grad, 1, 0)
-        acc[0] = key_grad * scale
-        acc[1] = value_grad
-
-        @pl.when((shard >= z) & (z > 0) & (tile < tiles - 1))
-        def _():
-            arrived(up_in.at[tile + 1], up_got.at[tile + 1])
-            acc[...] += up_in[tile + 1].astype(jnp.float32)
-
-        @pl.when((shard <= z) & (z < dp - 1) & (tile > 0))
-        def _():
-            arrived(down_in.at[tile - 1], down_got.at[tile - 1])
-            acc[...] += down_in[tile - 1].astype(jnp.float32)
-
-        @pl.when(shard == z)
-        def _():
-            owned[:, pl.ds(pl.multiple_of((index - z * blocks) * TILE, TILE), TILE), :] = acc[...].astype(jnp.bfloat16)
-
-        @pl.when(shard != z)
-        def _():
-            part[tile] = acc[...].astype(jnp.bfloat16)
-        part_copies(lambda c: c.start(), tile)
+        acc[tile, 0] = key_grad * scale
+        acc[tile, 1] = value_grad
+
+    def backward(i, carry):
+        @pl.when(i < tiles)
+        def _():
+            tile = place(i)
+            compute(tile)
+            above, below = waits_for(tile)
+
+            @pl.when(jnp.logical_not(above | below))
+            def _():
+                finish(tile)
+
+        @pl.when((i >= 1) & (i <= srv))
+        def _():
+            u = i - 1
+            att_out[u] = out_t[:, pl.ds(pl.multiple_of(u * wide, wide), wide)].T.astype(jnp.bfloat16)
+            att_copy(send, u)
+
+        @pl.when(i == tiles - 1)
+        def _():
+            for u in range(srv):
+                dq_out[u] = (dq_t[:, pl.ds(u * wide, wide)] * scale).T.astype(jnp.bfloat16)
+                dq_copy(send, u)
+
+        @pl.when(i >= LAG)
+        def _():
+            tile = place(i - LAG)
+            above, below = waits_for(tile)
+
+            @pl.when(above)
+            def _():
+                arrived(up_in.at[tile + 1], up_got.at[tile + 1])
+                acc[tile] += up_in[tile + 1].astype(jnp.float32)
+
+            @pl.when(below)
+            def _():
+                arrived(down_in.at[tile - 1], down_got.at[tile - 1])
+                acc[tile] += down_in[tile - 1].astype(jnp.float32)
+
+            @pl.when(above | below)
+            def _():
+                finish(tile)
         return carry
 
-    lax.fori_loop(0, tiles, backward, 0)
-
-    @pl.when((z > 0) & ((low_tile - 1) // blocks == z))
+    lax.fori_loop(0, tiles + LAG, backward, 0)
+
+    extra = (z > 0) & ((low_tile - 1) // blocks == z)
+    rest = jnp.minimum(jnp.maximum(low_tile - z * blocks, 0), blocks) * TILE
+
+    @pl.when(extra)
     def _():
         arrived(up_in.at[0], up_got.at[0])
-        owned[:, pl.ds(pl.multiple_of((low_tile - 1 - z * blocks) * TILE, TILE), TILE), :] = up_in[0]
-
-    def grad_copies(act):
-        column = pl.ds(pl.multiple_of(lane * HEAD_SIZE, HEAD_SIZE), HEAD_SIZE)
-        for j in range(lanes):
-            act(
-                lane == j,
-                owned.at[:, pl.ds(j * piece, piece), :],
-                g_ref.at[:, :, column],
-                g_sem.at[j],
-                g_got.at[lane],
-                (z, j // srv, j % srv),
-            )
-
-    grad_copies(send)
-    for u in range(srv):
-        dq_out[u] = (dq_t[:, pl.ds(u * wide, wide)] * scale).T.astype(jnp.bfloat16)
-        dq_copy(send, u)
+        owned[:, pl.ds(pl.multiple_of(rest - TILE, TILE), TILE), :] = up_in[0]
+
+    grad_copies(send, 0, rest)
 
     doc_copies(sent)
     key_copies(sent)
@@ -284,7 +334,7 @@
     for u in range(srv):
         dq_copy(sent, u)
         arrived(dq_ref.at[u], dq_got.at[u])
-    grad_copies(sent)
+    grad_copies(sent, 0, blocks * TILE)
     for j in range(lanes):
         arrived(g_ref.at[:, :, pl.ds(j * HEAD_SIZE, HEAD_SIZE)], g_got.at[j])
 
@@ -336,10 +386,9 @@
 
     both = jnp.stack([by_group(queries), by_group(output_gradient)], axis=1)
     docs = doc_ids.reshape(-1, TILE)
-    doc_rows = -(-docs.shape[0] // 8) * 8
-    docs = jnp.pad(docs, ((0, doc_rows - docs.shape[0]), (0, 0)))
     vmem = pl.BlockSpec(memory_space=pltpu.VMEM)
     anywhere = pl.BlockSpec(memory_space=pl.ANY)
+    outside = pl.BlockSpec(memory_space=pltpu.HBM)
     sem = pltpu.SemaphoreType.DMA
     lanes = heads * srv
     b16, f32 = jnp.bfloat16, jnp.float32
@@ -350,18 +399,20 @@
             jax.ShapeDtypeStruct((groups, wide, HEAD_SIZE), b16),
             jax.ShapeDtypeStruct((2, piece, lanes * HEAD_SIZE), b16),
         ),
-        in_specs=[anywhere] * 4,
+        in_specs=[anywhere, outside, outside, outside],
         out_specs=(vmem, vmem, vmem),
         scratch_shapes=[
             pltpu.VMEM((2, srv, wide, HEAD_SIZE), b16),
             pltpu.VMEM((tiles, 2, TILE, HEAD_SIZE), b16),
-            pltpu.VMEM((dp, doc_rows, TILE), jnp.int32),
+            pltpu.VMEM((dp, docs.shape[0], TILE), jnp.int32),
             pltpu.VMEM((tiles, TILE, srv * wide), f32),
+            pltpu.VMEM((1, srv * wide), f32),
             pltpu.VMEM((1, srv * wide), f32),
             pltpu.VMEM((1, srv * wide), f32),
             pltpu.VMEM((HEAD_SIZE, srv * wide), f32),
             pltpu.VMEM((HEAD_SIZE, srv * wide), f32),
-            pltpu.VMEM((2, TILE, HEAD_SIZE), f32),
+            pltpu.VMEM((HEAD_SIZE, srv * wide), f32),
+            pltpu.VMEM((tiles, 2, TILE, HEAD_SIZE), f32),
             pltpu.VMEM((tiles, 2, TILE, HEAD_SIZE), b16),
             pltpu.VMEM((tiles, 2, TILE, HEAD_SIZE), b16),
             pltpu.VMEM((tiles, 2, TILE, HEAD_SIZE), b16),

time: 59.7 us -> 56.2 us (0.941)
  Pallas kernels: 51.2 us -> 49 us
  local copies, waits for them, and re-layouts: 6.89 us -> 6.2 us
    pallas_call x1, Pallas kernels: 51.2 us -> 49 us  [local_window(): pl.pallas_call(functools.partial(attend, sizes), out_shape=(jax.ShapeDtyp...]
    pad x1 -> x0, local copies, waits for them, and re-layouts: 0.69 us -> none  [local_window(): docs = jnp.pad(docs, ((0, doc_rows - docs.shape[0]), (0, 0)))]
    unnamed x6 -> x8, local copies, waits for them, and re-layouts: 2.08 us -> 2.08 us
where the time goes in v3:
time: 56.2 us; the launch traced here: 56 us
  Pallas kernels  49 us (87%)
  local copies, waits for them, and re-layouts  6.2 us (11%)
  between operations  0.71 us (1%)
    pallas_call x1, Pallas kernels, local_window(): pl.pallas_call(functools.partial(attend, sizes), out_shape=(jax.ShapeDtyp...  49 us
    unnamed x8, local copies, waits for them, and re-layouts  2.08 us
    reshape x2, local copies, waits for them, and re-layouts, by_row(): array.reshape(groups, pair, home, HEAD_SIZE).transpose(2, 1, 0, 3)  1.61 us
    reshape x4, local copies, waits for them, and re-layouts, by_group(): array.reshape(home, pair, groups, HEAD_SIZE).transpose(2, 1, 0, 3)  1.36 us

profile of v3, /device:TPU:13, one launch (start us, length us, event | category | flops | bytes accessed | tf_op | source)
XLA Modules:
  0.0 56.0 jit_solution(10722601420607270484)
XLA Ops:
  0.6 1.1 %reshape.29 = bf16[128,2,4,128]{3,2,1,0:T(4,128)(2,1)S(1)} reshape(bf16[128,2,512]{2,1,0:T(2,128)(2,1)} %param.5) | data formatting | bytes 524288 | tf_op jit(solution)/shard_map/reshape | solution.py:385
  1.8 0.0 copy-start.3
  1.8 0.9 %copy-done.3 = bf16[128,2,512]{2,1,0:T(2,128)(2,1)S(1)} copy-done((bf16[128,2,512]{2,1,0:T(2,128)(2,1)S(1)}, bf16[128,2,512]{2,1,0:T(2,128)(2,1)}, u32[]{:S(2)}) %copy-start.3) | copy-done | bytes 262168
  2.7 0.2 reshape.30
  2.9 0.0 copy-start.1
  2.9 0.0 copy-start
  2.9 0.0 copy-start.2
  3.0 0.1 pad_maximum_fusion.qd_ref
  3.0 0.9 %copy-done.1 = bf16[320,1024]{1,0:T(8,128)(2,1)S(1)} copy-done((bf16[320,1024]{1,0:T(8,128)(2,1)S(1)}, bf16[320,1024]{1,0:T(8,128)(2,1)}, u32[]{:S(2)}) %copy-start.1) | copy-done | bytes 655384
  4.0 0.2 copy-done
  4.2 0.0 copy-done.2
  4.2 49.0 %shard_map.84 = (bf16[4,256,128]{2,1,0:T(8,128)(2,1)S(1)}, bf16[4,256,128]{2,1,0:T(8,128)(2,1)S(1)}, bf16[2,80,1024]{2,1,0:T(8,128)(2,1)S(1)}) custom-call(bf16[4,2,256,128]{3,2,1,0:T(8,128)(2,1)S(1)} %pad_maximum_fusion.qd_ref, bf16[320,1024]{1,0:T(8,128)(2,1)S(1)} %copy-done, bf16[320,1024]{1,0:T(8,128)(2,1)S(1)} %copy-done.1, s32[5,128]{1,0:T(8,128)S(1)} %bitcast.19), custom_call_target="tpu_custom_call" | custom-call | tf_op jit(solution)/shard_map/pallas_call | solution.py:395
  53.2 0.2 copy.11
  53.4 0.8 %reshape.33 = bf16[128,2,512]{2,1,0:T(2,128)(2,1)} reshape(bf16[128,2,4,128]{3,2,1,0:T(4,128)(2,1)S(1)} %copy.11) | data formatting | bytes 524288 | tf_op jit(solution)/shard_map/reshape | solution.py:436
  54.2 0.2 copy.12
  54.4 0.8 %reshape.35 = bf16[128,2,512]{2,1,0:T(2,128)(2,1)} reshape(bf16[128,2,4,128]{3,2,1,0:T(4,128)(2,1)S(1)} %copy.12) | data formatting | bytes 524288 | tf_op jit(solution)/shard_map/reshape | solution.py:436
  55.2 0.7 %slice_bitcast_fusion = (bf16[80,1024]{1,0:T(8,128)(2,1)}, bf16[80,1024]{1,0:T(8,128)(2,1)}) fusion(bf16[2,80,1024]{2,1,0:T(8,128)(2,1)S(1)} %get-tuple-element.9), kind=kLoop, calls=%fused_computation.1 | loop fusion | bytes 655360 | tf_op jit(solution)/shard_map/squeeze | solution.py:438
  (2 shorter events, 0.1 us)
Async XLA Ops:
  1.8 1.0 %copy-start.3 = (bf16[128,2,512]{2,1,0:T(2,128)(2,1)S(1)}, bf16[128,2,512]{2,1,0:T(2,128)(2,1)}, u32[]{:S(2)}) copy-start(bf16[128,2,512]{2,1,0:T(2,128)(2,1)} %param.8) | copy-start | bytes 786436
  2.9 1.1 %copy-start.1 = (bf16[320,1024]{1,0:T(8,128)(2,1)S(1)}, bf16[320,1024]{1,0:T(8,128)(2,1)}, u32[]{:S(2)}) copy-start(bf16[320,1024]{1,0:T(8,128)(2,1)} %v_ref.1) | copy-start | bytes 1966084
  2.9 1.2 %copy-start = (bf16[320,1024]{1,0:T(8,128)(2,1)S(1)}, bf16[320,1024]{1,0:T(8,128)(2,1)}, u32[]{:S(2)}) copy-start(bf16[320,1024]{1,0:T(8,128)(2,1)} %k_ref.1) | copy-start | bytes 1966084
  2.9 1.2 %copy-start.2 = (s32[640]{0:T(1024)S(1)}, s32[640]{0:T(1024)}, u32[]{:S(2)}) copy-start(s32[640]{0:T(1024)} %param.9) | copy-start | bytes 7684

commit v4 on v3

--- a/solution.py
+++ b/solution.py
@@ -17,16 +17,16 @@
 
 
 TILE = 128
+HALF = 64
 LAG = 3
-
-
-def attend(sizes, qd_ref, k_ref, v_ref, doc_ref, att_ref, dq_ref, g_ref,
-           qd_buf, kv_buf, docs, scores, top, norm, delta, out_t, grad_t, dq_t, acc, part, up_in, down_in, owned, att_out, dq_out,
-           q_sem, q_got, kv_sem, kv_got, relay_sem, doc_sem, doc_got, att_sem, att_got, dq_sem, dq_got,
+AHEAD = 3
+
+
+def attend(sizes, q_ref, o_ref, k_ref, v_ref, doc_ref, att_ref, dq_ref, g_ref,
+           raw, stage, qd_buf, kv_buf, docs, scores, top, norm, delta, out_t, grad_t, dq_t, acc, part, up_in, down_in, owned, att_out, dq_out,
+           raw_got, q_sem, q_got, kv_sem, kv_got, relay_sem, doc_sem, doc_got, att_sem, att_got, dq_sem, dq_got,
            part_sem, up_got, down_got, g_sem, g_got):
     dp, heads, srv, home, pair, rows, first, window = sizes
-    chunk = math.gcd(TILE, rows)
-    chunks = rows // chunk
     piece = rows // srv
     wide = pair * home
     every = srv * wide
@@ -65,6 +65,17 @@
     def arrived(ref, sem):
         pltpu.make_async_copy(ref, ref, sem).wait()
 
+    for which, ref in ((0, q_ref), (1, o_ref)):
+        pltpu.make_async_copy(ref, raw.at[which], raw_got.at[which]).start()
+
+    def stage_queries():
+        for which in range(2):
+            arrived(raw.at[which], raw_got.at[which])
+            for u in range(srv):
+                block = raw[which, :, :, pl.ds(u * HEAD_SIZE, HEAD_SIZE)].astype(jnp.float32)
+                for j in range(pair):
+                    stage[u, which, pl.ds(j * home, home), :] = block[:, j, :].astype(jnp.bfloat16)
+
     barrier = pltpu.get_barrier_semaphore()
 
     def greet(index, carry):
@@ -84,28 +95,30 @@
 
     def key_copies(act):
         def one(index, carry):
-            side, h = index // heads, index % heads
-            s = z + jnp.where(side == 0, -1, jnp.where(side == 1, 1, 0))
+            side, h = index // heads, (x + index) % heads
+            s = z + side - 1
             column = pl.ds(pl.multiple_of((h * srv + v) * HEAD_SIZE, HEAD_SIZE), HEAD_SIZE)
             start = first + home * s
 
-            def each(c, inner):
-                row = base + c * chunk - start
+            def each(at, count, slot):
+                row = base + at - start
 
                 @pl.when((s >= 0) & (s < dp) & (row >= 0) & (row < window))
                 def _():
                     for which, ref in ((0, k_ref), (1, v_ref)):
                         act(
                             (s == z) & (h == x),
-                            ref.at[pl.ds(pl.multiple_of(c * chunk, chunk), chunk), column],
-                            kv_buf.at[row // TILE, which, pl.ds(pl.multiple_of(row % TILE, chunk), chunk), :],
-                            kv_sem.at[index, c, which],
+                            ref.at[pl.ds(pl.multiple_of(at, HALF), count), column],
+                            kv_buf.at[row // TILE, which, pl.ds(pl.multiple_of(row % TILE, count), count), :],
+                            kv_sem.at[index, slot, which],
                             kv_got.at[row // TILE],
                             (s, h, v),
                         )
-                return inner
-
-            lax.fori_loop(0, chunks, each, 0)
+
+            for c in range(rows // TILE):
+                each(c * TILE + base % TILE, TILE, c)
+            if rows % TILE:
+                each(jnp.where(base % TILE == 0, rows - HALF, 0), HALF, rows // TILE)
             return carry
 
         lax.fori_loop(0, 3 * heads, one, 0)
@@ -116,11 +129,12 @@
 
     def query_copies(act):
         for u in range(srv):
-            act(v == u, qd_ref.at[u], qd_buf.at[:, v], q_sem.at[u], q_got.at[v], (z, x, u))
-
+            act(v == u, stage.at[u], qd_buf.at[:, v], q_sem.at[u], q_got.at[v], (z, x, u))
+
+    key_copies(send)
     doc_copies(send)
+    stage_queries()
     query_copies(send)
-    key_copies(send)
 
     top[...] = jnp.full_like(top, NEGATIVE / 10)
     norm[...] = jnp.zeros_like(norm)
@@ -155,11 +169,25 @@
         def _():
             act(copy(kv_buf.at[tile], kv_buf.at[tile - 1], relay_sem.at[tile], kv_got.at[tile - 1], (z + 1, x, v)))
 
+    ahead = jnp.where((z > 0) & (z < dp - 1), AHEAD, 0)
+
     def forward(i, carry):
-        tile = jnp.where(i < tiles - own_first, own_first + i, tiles - 1 - i)
+        def turn(i):
+            return jnp.where(i < tiles - own_first, own_first + i, tiles - 1 - i)
+
+        @pl.when(i < tiles)
+        def _():
+            tile = turn(i)
+            arrived(kv_buf.at[tile], kv_got.at[tile])
+            relays(lambda c: c.start(), tile)
+
+        @pl.when((i >= ahead) & (i < tiles + ahead))
+        def _():
+            meet(turn(i - ahead))
+        return carry
+
+    def meet(tile):
         index = low_tile + tile
-        arrived(kv_buf.at[tile], kv_got.at[tile])
-        relays(lambda c: c.start(), tile)
         key_doc = docs[index // blocks, pl.ds(index % blocks, 1), :]
         key_doc = jnp.broadcast_to(key_doc.astype(jnp.float32), (TILE, TILE)).T
         key_at = lax.broadcasted_iota(jnp.int32, (TILE, home), 0) + index * TILE
@@ -177,9 +205,8 @@
             top[:, at] = new
             norm[:, at] = norm[:, at] * shrink + jnp.sum(weights, axis=0, keepdims=True)
             out_t[:, at] = out_t[:, at] * shrink + contract(value_t, weights.astype(jnp.bfloat16), 1, 0)
-        return carry
-
-    lax.fori_loop(0, tiles, forward, 0)
+
+    lax.fori_loop(0, tiles + AHEAD, forward, 0)
 
     def att_copy(act, u):
         act(v == u, att_out.at[u], att_ref.at[v], att_sem.at[u], att_got.at[v], (z, x, u))
@@ -306,17 +333,18 @@
                 finish(tile)
         return carry
 
-    lax.fori_loop(0, tiles + LAG, backward, 0)
-
     extra = (z > 0) & ((low_tile - 1) // blocks == z)
     rest = jnp.minimum(jnp.maximum(low_tile - z * blocks, 0), blocks) * TILE
+    idle = jnp.where(extra, jnp.maximum(rest - TILE - piece + 1, 0), rest)
+    grad_copies(send, 0, idle)
+    lax.fori_loop(0, tiles + LAG, backward, 0)
 
     @pl.when(extra)
     def _():
         arrived(up_in.at[0], up_got.at[0])
         owned[:, pl.ds(pl.multiple_of(rest - TILE, TILE), TILE), :] = up_in[0]
 
-    grad_copies(send, 0, rest)
+    grad_copies(send, idle, rest)
 
     doc_copies(sent)
     key_copies(sent)
@@ -354,7 +382,7 @@
     shard = rows * heads
     if width != srv * HEAD_SIZE or home != TILE or shard % TILE or first < 0 or first % TILE or window % TILE:
         return False
-    if rows % srv or (rows // srv) % 16 or rows % 16:
+    if rows % HALF or rows % srv or (rows // srv) % 16 or rows % 16:
         return False
     blocks, tiles, start = shard // TILE, window // TILE, first // TILE
     for s in range(dp):
@@ -379,15 +407,10 @@
     wide = pair * home
     tiles = window // TILE
     piece = rows // srv
-    chunks = rows // math.gcd(TILE, rows)
-
-    def by_group(array):
-        return array.reshape(home, pair, groups, HEAD_SIZE).transpose(2, 1, 0, 3).reshape(groups, wide, HEAD_SIZE)
-
-    both = jnp.stack([by_group(queries), by_group(output_gradient)], axis=1)
+    chunks = -(-rows // TILE)
+
     docs = doc_ids.reshape(-1, TILE)
     vmem = pl.BlockSpec(memory_space=pltpu.VMEM)
-    anywhere = pl.BlockSpec(memory_space=pl.ANY)
     outside = pl.BlockSpec(memory_space=pltpu.HBM)
     sem = pltpu.SemaphoreType.DMA
     lanes = heads * srv
@@ -399,9 +422,11 @@
             jax.ShapeDtypeStruct((groups, wide, HEAD_SIZE), b16),
             jax.ShapeDtypeStruct((2, piece, lanes * HEAD_SIZE), b16),
         ),
-        in_specs=[anywhere, outside, outside, outside],
+        in_specs=[outside] * 5,
         out_specs=(vmem, vmem, vmem),
         scratch_shapes=[
+            pltpu.VMEM((2, home, pair, width), b16),
+            pltpu.VMEM((srv, 2, wide, HEAD_SIZE), b16),
             pltpu.VMEM((2, srv, wide, HEAD_SIZE), b16),
             pltpu.VMEM((tiles, 2, TILE, HEAD_SIZE), b16),
             pltpu.VMEM((dp, docs.shape[0], TILE), jnp.int32),
@@ -419,7 +444,7 @@
             pltpu.VMEM((2, rows * heads, HEAD_SIZE), b16),
             pltpu.VMEM((srv, wide, HEAD_SIZE), b16),
             pltpu.VMEM((srv, wide, HEAD_SIZE), b16),
-            sem((srv,)), sem((srv,)),
+            sem((2,)), sem((srv,)), sem((srv,)),
             sem((3 * heads, chunks, 2)), sem((tiles,)), sem((tiles,)),
             sem((dp,)), sem((dp,)),
             sem((srv,)), sem((srv,)),
@@ -428,9 +453,9 @@
             sem((lanes,)), sem((lanes,)),
         ],
         compiler_params=pltpu.CompilerParams(
-            collective_id=0, has_side_effects=True, vmem_limit_bytes=40 * 1024 * 1024
+            collective_id=0, has_side_effects=True, vmem_limit_bytes=63 * 1024 * 1024
         ),
-    )(both, keys, values, docs)
+    )(queries, output_gradient, keys, values, docs)
 
     def by_row(array):
         return array.reshape(groups, pair, home, HEAD_SIZE).transpose(2, 1, 0, 3).reshape(home, pair, width)

time: 56.2 us -> 54.8 us (0.975)
  local copies, waits for them, and re-layouts: 6.2 us -> 4.01 us
  Pallas kernels: 49 us -> 49.9 us
    unnamed x8 -> x4, local copies, waits for them, and re-layouts: 2.08 us -> 0.3 us
    reshape x4 -> x0, local copies, waits for them, and re-layouts: 1.36 us -> none  [by_group(): array.reshape(home, pair, groups, HEAD_SIZE).transpose(2, 1, 0, 3)]
    transpose x2, local copies, waits for them, and re-layouts: 0.41 us -> 1.36 us  [by_row(): array.reshape(groups, pair, home, HEAD_SIZE).transpose(2, 1, 0, 3)]
    pallas_call x1, Pallas kernels: 49 us -> 49.9 us  [local_window(): pl.pallas_call(functools.partial(attend, sizes), out_shape=(jax.ShapeDtyp...]
where the time goes in v4:
time: 54.8 us; the launch traced here: 54.6 us
  Pallas kernels  49.9 us (91%)
  local copies, waits for them, and re-layouts  4.01 us (7%)
  between operations  0.66 us (1%)
    pallas_call x1, Pallas kernels, local_window(): pl.pallas_call(functools.partial(attend, sizes), out_shape=(jax.ShapeDtyp...  49.9 us
    reshape x2, local copies, waits for them, and re-layouts, by_row(): array.reshape(groups, pair, home, HEAD_SIZE).transpose(2, 1, 0, 3)  1.61 us
    transpose x2, local copies, waits for them, and re-layouts, by_row(): array.reshape(groups, pair, home, HEAD_SIZE).transpose(2, 1, 0, 3)  1.36 us

profile of v4, /device:TPU:13, one launch (start us, length us, event | category | flops | bytes accessed | tf_op | source)
XLA Modules:
  0.0 54.6 jit_solution(17196331701017942962)
XLA Ops:
  0.6 49.9 %shard_map.84 = (bf16[4,256,128]{2,1,0:T(8,128)(2,1)}, bf16[4,256,128]{2,1,0:T(8,128)(2,1)}, bf16[2,80,1024]{2,1,0:T(8,128)(2,1)}) custom-call(bf16[128,2,512]{2,1,0:T(2,128)(2,1)} %q_ref.1, bf16[128,2,512]{2,1,0:T(2,128)(2,1)} %o_ref.1, bf16[320,1024]{1,0:T(8,128)(2,1)} %k_ref.1, bf16[320,1024]{1,0:T(8,128)(2,1)} %v_ref.1, s32[5,128]{1,0:T(8,128)} %bitcast.13), custom_call_target="tpu_custom_call" | custom-call | tf_op jit(solution)/shard_map/pallas_call | solution.py:418
  50.5 1.2 %copy.9 = bf16[128,2,4,128]{3,2,1,0:T(4,128)(2,1)S(1)} copy(bf16[128,2,4,128]{3,0,1,2:T(8,128)(2,1)} %bitcast.12) | data formatting | bytes 524288 | tf_op jit(solution)/shard_map/transpose | solution.py:461
  51.7 0.0 copy-start.1
  51.7 0.8 %reshape.25 = bf16[128,2,512]{2,1,0:T(2,128)(2,1)} reshape(bf16[128,2,4,128]{3,2,1,0:T(4,128)(2,1)S(1)} %copy.9) | data formatting | bytes 524288 | tf_op jit(solution)/shard_map/reshape | solution.py:461
  52.5 0.1 copy-done.1
  52.6 0.2 copy.10
  52.8 0.0 copy-start
  52.9 0.8 %reshape.27 = bf16[128,2,512]{2,1,0:T(2,128)(2,1)} reshape(bf16[128,2,4,128]{3,2,1,0:T(4,128)(2,1)S(1)} %copy.10) | data formatting | bytes 524288 | tf_op jit(solution)/shard_map/reshape | solution.py:461
  53.7 0.2 copy-done
  53.8 0.7 %slice_bitcast_fusion = (bf16[80,1024]{1,0:T(8,128)(2,1)}, bf16[80,1024]{1,0:T(8,128)(2,1)}) fusion(bf16[2,80,1024]{2,1,0:T(8,128)(2,1)S(1)} %copy-done), kind=kLoop, calls=%fused_computation | loop fusion | bytes 655360 | tf_op jit(solution)/shard_map/squeeze | solution.py:463
Async XLA Ops:
  51.7 1.0 %copy-start.1 = (bf16[4,256,128]{2,1,0:T(8,128)(2,1)S(1)}, bf16[4,256,128]{2,1,0:T(8,128)(2,1)}, u32[]{:S(2)}) copy-start(bf16[4,256,128]{2,1,0:T(8,128)(2,1)} %get-tuple-element.8) | copy-start | bytes 786436
  52.8 1.0 %copy-start = (bf16[2,80,1024]{2,1,0:T(8,128)(2,1)S(1)}, bf16[2,80,1024]{2,1,0:T(8,128)(2,1)}, u32[]{:S(2)}) copy-start(bf16[2,80,1024]{2,1,0:T(8,128)(2,1)} %get-tuple-element.9) | copy-start | bytes 983044

commit v5 on v4

--- a/solution.py
+++ b/solution.py
@@ -23,7 +23,7 @@
 
 
 def attend(sizes, q_ref, o_ref, k_ref, v_ref, doc_ref, att_ref, dq_ref, g_ref,
-           raw, stage, qd_buf, kv_buf, docs, scores, top, norm, delta, out_t, grad_t, dq_t, acc, part, up_in, down_in, owned, att_out, dq_out,
+           raw, stage, qd_buf, kv_buf, docs, scores, top, norm, delta, out_t, grad_t, dq_t, acc, part, up_in, down_in, owned, att_out, dq_out, att_in, dq_in,
            raw_got, q_sem, q_got, kv_sem, kv_got, relay_sem, doc_sem, doc_got, att_sem, att_got, dq_sem, dq_got,
            part_sem, up_got, down_got, g_sem, g_got):
     dp, heads, srv, home, pair, rows, first, window = sizes
@@ -75,6 +75,10 @@
                 block = raw[which, :, :, pl.ds(u * HEAD_SIZE, HEAD_SIZE)].astype(jnp.float32)
                 for j in range(pair):
                     stage[u, which, pl.ds(j * home, home), :] = block[:, j, :].astype(jnp.bfloat16)
+
+    def by_row(source, target, u):
+        heads_of = [source[u, pl.ds(j * home, home), :].astype(jnp.float32) for j in range(pair)]
+        target[:, :, pl.ds(u * HEAD_SIZE, HEAD_SIZE)] = jnp.stack(heads_of, axis=1).astype(jnp.bfloat16)
 
     barrier = pltpu.get_barrier_semaphore()
 
@@ -209,10 +213,10 @@
     lax.fori_loop(0, tiles + AHEAD, forward, 0)
 
     def att_copy(act, u):
-        act(v == u, att_out.at[u], att_ref.at[v], att_sem.at[u], att_got.at[v], (z, x, u))
+        act(v == u, att_out.at[u], att_in.at[v], att_sem.at[u], att_got.at[v], (z, x, u))
 
     def dq_copy(act, u):
-        act(v == u, dq_out.at[u], dq_ref.at[v], dq_sem.at[u], dq_got.at[v], (z, x, u))
+        act(v == u, dq_out.at[u], dq_in.at[v], dq_sem.at[u], dq_got.at[v], (z, x, u))
 
     for u in range(srv):
         at = pl.ds(u * wide, wide)
@@ -250,8 +254,15 @@
 
         lax.fori_loop(0, lanes, one, 0)
 
+    above_first = (low_tile // blocks == z + 1) & (low_tile % blocks > 0)
+
     def place(i):
-        return jnp.where(i == 0, tiles - 1, jnp.where(i <= own_first, i - 1, tiles - 1 + own_first - i))
+        tile = jnp.where(i == 0, tiles - 1, jnp.where(i <= own_first, i - 1, tiles - 1 + own_first - i))
+        return jnp.where(above_first & (i >= tiles - 2), 1 - tile, tile)
+
+    extra = (z > 0) & ((low_tile - 1) // blocks == z)
+    rest = jnp.minimum(jnp.maximum(low_tile - z * blocks, 0), blocks) * TILE
+    idle = jnp.where(extra, jnp.maximum(rest - TILE - piece + 1, 0), rest)
 
     def waits_for(tile):
         shard = (low_tile + tile) // blocks
@@ -267,7 +278,7 @@
         def _():
             row = (index - z * blocks) * TILE
             owned[:, pl.ds(pl.multiple_of(row, TILE), TILE), :] = acc[tile].astype(jnp.bfloat16)
-            grad_copies(send, row, row + TILE)
+            grad_copies(send, jnp.where(extra & (row == rest), rest - piece + 1, row), row + TILE)
 
         @pl.when(shard != z)
         def _():
@@ -318,6 +329,12 @@
             tile = place(i - LAG)
             above, below = waits_for(tile)
 
+            @pl.when(extra & (i - LAG == tiles - 1))
+            def _():
+                arrived(up_in.at[0], up_got.at[0])
+                owned[:, pl.ds(pl.multiple_of(rest - TILE, TILE), TILE), :] = up_in[0]
+                grad_copies(send, idle, rest - piece + 1)
+
             @pl.when(above)
             def _():
                 arrived(up_in.at[tile + 1], up_got.at[tile + 1])
@@ -333,19 +350,16 @@
                 finish(tile)
         return carry
 
-    extra = (z > 0) & ((low_tile - 1) // blocks == z)
-    rest = jnp.minimum(jnp.maximum(low_tile - z * blocks, 0), blocks) * TILE
-    idle = jnp.where(extra, jnp.maximum(rest - TILE - piece + 1, 0), rest)
     grad_copies(send, 0, idle)
     lax.fori_loop(0, tiles + LAG, backward, 0)
 
-    @pl.when(extra)
-    def _():
-        arrived(up_in.at[0], up_got.at[0])
-        owned[:, pl.ds(pl.multiple_of(rest - TILE, TILE), TILE), :] = up_in[0]
-
-    grad_copies(send, idle, rest)
-
+
+    for u in range(srv):
+        arrived(att_in.at[u], att_got.at[u])
+        by_row(att_in, att_ref, u)
+    for u in range(srv):
+        arrived(dq_in.at[u], dq_got.at[u])
+        by_row(dq_in, dq_ref, u)
     doc_copies(sent)
     key_copies(sent)
     query_copies(sent)
@@ -358,10 +372,7 @@
     lax.fori_loop(0, tiles, settle, 0)
     for u in range(srv):
         att_copy(sent, u)
-        arrived(att_ref.at[u], att_got.at[u])
-    for u in range(srv):
         dq_copy(sent, u)
-        arrived(dq_ref.at[u], dq_got.at[u])
     grad_copies(sent, 0, blocks * TILE)
     for j in range(lanes):
         arrived(g_ref.at[:, :, pl.ds(j * HEAD_SIZE, HEAD_SIZE)], g_got.at[j])
@@ -403,7 +414,6 @@
 def local_window(sizes, queries, keys, values, output_gradient, doc_ids):
     dp, heads, srv, home, pair, rows, first, window = sizes
     width = queries.shape[2]
-    groups = width // HEAD_SIZE
     wide = pair * home
     tiles = window // TILE
     piece = rows // srv
@@ -418,8 +428,8 @@
     att, dq, kv = pl.pallas_call(
         functools.partial(attend, sizes),
         out_shape=(
-            jax.ShapeDtypeStruct((groups, wide, HEAD_SIZE), b16),
-            jax.ShapeDtypeStruct((groups, wide, HEAD_SIZE), b16),
+            jax.ShapeDtypeStruct((home, pair, width), b16),
+            jax.ShapeDtypeStruct((home, pair, width), b16),
             jax.ShapeDtypeStruct((2, piece, lanes * HEAD_SIZE), b16),
         ),
         in_specs=[outside] * 5,
@@ -444,6 +454,8 @@
             pltpu.VMEM((2, rows * heads, HEAD_SIZE), b16),
             pltpu.VMEM((srv, wide, HEAD_SIZE), b16),
             pltpu.VMEM((srv, wide, HEAD_SIZE), b16),
+            pltpu.VMEM((srv, wide, HEAD_SIZE), b16),
+            pltpu.VMEM((srv, wide, HEAD_SIZE), b16),
             sem((2,)), sem((srv,)), sem((srv,)),
             sem((3 * heads, chunks, 2)), sem((tiles,)), sem((tiles,)),
             sem((dp,)), sem((dp,)),
@@ -457,10 +469,7 @@
         ),
     )(queries, output_gradient, keys, values, docs)
 
-    def by_row(array):
-        return array.reshape(groups, pair, home, HEAD_SIZE).transpose(2, 1, 0, 3).reshape(home, pair, width)
-
-    return by_row(att), by_row(dq), kv[0], kv[1]
+    return att, dq, kv[0], kv[1]
 
 
 def local_spread(queries, keys, values, output_gradient, doc_ids):

time: 54.8 us -> 53.5 us (0.976)
  Pallas kernels: 49.9 us -> 49.2 us
    reshape x2 -> x0, local copies, waits for them, and re-layouts: 1.61 us -> none  [by_row(): array.reshape(groups, pair, home, HEAD_SIZE).transpose(2, 1, 0, 3)]
    unnamed x4 -> x6, local copies, waits for them, and re-layouts: 0.3 us -> 1.75 us
    transpose x2 -> x0, local copies, waits for them, and re-layouts: 1.36 us -> none  [by_row(): array.reshape(groups, pair, home, HEAD_SIZE).transpose(2, 1, 0, 3)]
    squeeze x1, local copies, waits for them, and re-layouts: 0.74 us -> 1.78 us  [local_window(): return (att, dq, kv[0], kv[1])]
    pallas_call x1, Pallas kernels: 49.9 us -> 49.2 us  [local_window(): pl.pallas_call(functools.partial(attend, sizes), out_shape=(jax.ShapeDtyp...]
where the time goes in v5:
time: 53.5 us; the launch traced here: 53.4 us
  Pallas kernels  49.2 us (92%)
  local copies, waits for them, and re-layouts  3.53 us (7%)
  between operations  0.65 us (1%)
    pallas_call x1, Pallas kernels, local_window(): pl.pallas_call(functools.partial(attend, sizes), out_shape=(jax.ShapeDtyp...  49.2 us
    squeeze x1, local copies, waits for them, and re-layouts, local_window(): return (att, dq, kv[0], kv[1])  1.78 us
    unnamed x6, local copies, waits for them, and re-layouts  1.75 us

profile of v5, /device:TPU:13, one launch (start us, length us, event | category | flops | bytes accessed | tf_op | source)
XLA Modules:
  0.0 53.4 jit_solution(8737246168226493977)
XLA Ops:
  0.6 49.2 %shard_map.84 = (bf16[128,2,512]{2,1,0:T(2,128)(2,1)}, bf16[128,2,512]{2,1,0:T(2,128)(2,1)}, bf16[2,80,1024]{2,1,0:T(8,128)(2,1)}) custom-call(bf16[128,2,512]{2,1,0:T(2,128)(2,1)} %q_ref.1, bf16[128,2,512]{2,1,0:T(2,128)(2,1)} %o_ref.1, bf16[320,1024]{1,0:T(8,128)(2,1)} %k_ref.1, bf16[320,1024]{1,0:T(8,128)(2,1)} %v_ref.1, s32[5,128]{1,0:T(8,128)} %bitcast.5), custom_call_target="tpu_custom_call" | custom-call | tf_op jit(solution)/shard_map/pallas_call | solution.py:428
  49.8 0.0 copy-start.1
  49.8 1.8 %slice_bitcast_fusion = (bf16[80,1024]{1,0:T(8,128)(2,1)}, bf16[80,1024]{1,0:T(8,128)(2,1)}) fusion(bf16[2,80,1024]{2,1,0:T(8,128)(2,1)} %get-tuple-element.9), kind=kLoop, calls=%fused_computation | loop fusion | bytes 655360 | tf_op jit(solution)/shard_map/squeeze | solution.py:472
  51.6 0.0 copy-done.1
  51.6 0.0 copy-start
  51.6 0.7 %copy.11 = bf16[128,2,512]{2,1,0:T(2,128)(2,1)} copy(bf16[128,2,512]{2,1,0:T(2,128)(2,1)S(1)} %copy-done.1) | data formatting | bytes 524288
  52.3 0.3 copy-done
  52.7 0.7 %copy.12 = bf16[128,2,512]{2,1,0:T(2,128)(2,1)} copy(bf16[128,2,512]{2,1,0:T(2,128)(2,1)S(1)} %copy-done) | data formatting | bytes 524288
Async XLA Ops:
  49.8 1.8 %copy-start.1 = (bf16[128,2,512]{2,1,0:T(2,128)(2,1)S(1)}, bf16[128,2,512]{2,1,0:T(2,128)(2,1)}, u32[]{:S(2)}) copy-start(bf16[128,2,512]{2,1,0:T(2,128)(2,1)} %get-tuple-element.16) | copy-start | bytes 786436
  51.6 1.0 %copy-start = (bf16[128,2,512]{2,1,0:T(2,128)(2,1)S(1)}, bf16[128,2,512]{2,1,0:T(2,128)(2,1)}, u32[]{:S(2)}) copy-start(bf16[128,2,512]{2,1,0:T(2,128)(2,1)} %get-tuple-element.17) | copy-start | bytes 786436

commit v6 on v5

--- a/solution.py
+++ b/solution.py
@@ -82,18 +82,22 @@
 
     barrier = pltpu.get_barrier_semaphore()
 
-    def greet(index, carry):
-        s, h, u = index // lanes, (index // srv) % heads, index % srv
-        beside = (s - z == 1) | (z - s == 1)
-        partner = (s == z) | ((u == v) & (beside | (h == x)))
-        myself = (s == z) & (h == x) & (u == v)
-
-        @pl.when(partner & jnp.logical_not(myself))
-        def _():
-            pl.semaphore_signal(barrier, inc=1, device_id=(s, h, u), device_id_type=MESH)
-        return carry
-
-    lax.fori_loop(0, dp * lanes, greet, 0)
+    def greet(s, h, u):
+        pl.semaphore_signal(barrier, inc=1, device_id=(s, h, u), device_id_type=MESH)
+
+    for step in range(1, dp):
+        greet((z + step) % dp, x, v)
+    for step in range(1, heads):
+        @pl.when(z > 0)
+        def _():
+            greet(z - 1, (x + step) % heads, v)
+
+        @pl.when(z < dp - 1)
+        def _():
+            greet(z + 1, (x + step) % heads, v)
+    for step in range(1, lanes):
+        other = (lane + step) % lanes
+        greet(z, other // srv, other % srv)
     sides = jnp.where(z > 0, 1, 0) + jnp.where(z < dp - 1, 1, 0)
     pl.semaphore_wait(barrier, lanes - 1 + sides * heads + dp - 1 - sides)
 
@@ -288,18 +292,17 @@
     def compute(tile):
         key_t = turned(kv_buf[tile, 0])
         values = kv_buf[tile, 1]
-        key_grad = jnp.zeros((TILE, HEAD_SIZE), jnp.float32)
-        value_grad = jnp.zeros((TILE, HEAD_SIZE), jnp.float32)
+        all_probs, all_grads = [], []
         for u in range(srv):
             at = pl.ds(u * wide, wide)
             probs = jnp.exp2(scores[tile, :, at] * exponent - top[:, at])
             weight_grad = contract(values, qd_buf[1, u], 1, 1)
-            score_grad = (probs * (weight_grad - delta[:, at])).astype(jnp.bfloat16)
-            key_grad = key_grad + contract(score_grad, qd_buf[0, u], 1, 0)
-            value_grad = value_grad + contract(probs.astype(jnp.bfloat16), qd_buf[1, u], 1, 0)
-            dq_t[:, at] += contract(key_t, score_grad, 1, 0)
-        acc[tile, 0] = key_grad * scale
-        acc[tile, 1] = value_grad
+            all_grads.append((probs * (weight_grad - delta[:, at])).astype(jnp.bfloat16))
+            all_probs.append(probs.astype(jnp.bfloat16))
+            dq_t[:, at] += contract(key_t, all_grads[-1], 1, 0)
+        flat = (srv * wide, HEAD_SIZE)
+        acc[tile, 0] = contract(jnp.concatenate(all_grads, axis=1), qd_buf[0].reshape(flat), 1, 0) * scale
+        acc[tile, 1] = contract(jnp.concatenate(all_probs, axis=1), qd_buf[1].reshape(flat), 1, 0)
 
     def backward(i, carry):
         @pl.when(i < tiles)
@@ -323,6 +326,15 @@
             for u in range(srv):
                 dq_out[u] = (dq_t[:, pl.ds(u * wide, wide)] * scale).T.astype(jnp.bfloat16)
                 dq_copy(send, u)
+            for u in range(srv):
+                arrived(att_in.at[u], att_got.at[u])
+                by_row(att_in, att_ref, u)
+
+        @pl.when(i == tiles + LAG - 2)
+        def _():
+            for u in range(srv):
+                arrived(dq_in.at[u], dq_got.at[u])
+                by_row(dq_in, dq_ref, u)
 
         @pl.when(i >= LAG)
         def _():
@@ -354,12 +366,6 @@
     lax.fori_loop(0, tiles + LAG, backward, 0)
 
 
-    for u in range(srv):
-        arrived(att_in.at[u], att_got.at[u])
-        by_row(att_in, att_ref, u)
-    for u in range(srv):
-        arrived(dq_in.at[u], dq_got.at[u])
-        by_row(dq_in, dq_ref, u)
     doc_copies(sent)
     key_copies(sent)
     query_copies(sent)

time: 53.5 us -> 54.9 us (1.026)
  Pallas kernels: 49.2 us -> 50.2 us
    pallas_call x1, Pallas kernels: 49.2 us -> 50.2 us  [local_window(): pl.pallas_call(functools.partial(attend, sizes), out_shape=(jax.ShapeDtyp...]
where the time goes in v6:
time: 54.9 us; the launch traced here: 54.4 us
  Pallas kernels  50.2 us (91%)
  local copies, waits for them, and re-layouts  3.53 us (6%)
  between operations  0.65 us (1%)
    pallas_call x1, Pallas kernels, local_window(): pl.pallas_call(functools.partial(attend, sizes), out_shape=(jax.ShapeDtyp...  50.2 us
    squeeze x1, local copies, waits for them, and re-layouts, local_window(): return (att, dq, kv[0], kv[1])  1.78 us
    unnamed x6, local copies, waits for them, and re-layouts  1.75 us

profile of v6, /device:TPU:13, one launch (start us, length us, event | category | flops | bytes accessed | tf_op | source)
XLA Modules:
  0.0 54.4 jit_solution(4856703730049443428)
XLA Ops:
  0.6 50.2 %shard_map.84 = (bf16[128,2,512]{2,1,0:T(2,128)(2,1)}, bf16[128,2,512]{2,1,0:T(2,128)(2,1)}, bf16[2,80,1024]{2,1,0:T(8,128)(2,1)}) custom-call(bf16[128,2,512]{2,1,0:T(2,128)(2,1)} %q_ref.1, bf16[128,2,512]{2,1,0:T(2,128)(2,1)} %o_ref.1, bf16[320,1024]{1,0:T(8,128)(2,1)} %k_ref.1, bf16[320,1024]{1,0:T(8,128)(2,1)} %v_ref.1, s32[5,128]{1,0:T(8,128)} %bitcast.5), custom_call_target="tpu_custom_call" | custom-call | tf_op jit(solution)/shard_map/pallas_call | solution.py:434
  50.8 0.0 copy-start.1
  50.8 1.8 %slice_bitcast_fusion = (bf16[80,1024]{1,0:T(8,128)(2,1)}, bf16[80,1024]{1,0:T(8,128)(2,1)}) fusion(bf16[2,80,1024]{2,1,0:T(8,128)(2,1)} %get-tuple-element.9), kind=kLoop, calls=%fused_computation | loop fusion | bytes 655360 | tf_op jit(solution)/shard_map/squeeze | solution.py:478
  52.6 0.0 copy-done.1
  52.6 0.0 copy-start
  52.6 0.7 %copy.11 = bf16[128,2,512]{2,1,0:T(2,128)(2,1)} copy(bf16[128,2,512]{2,1,0:T(2,128)(2,1)S(1)} %copy-done.1) | data formatting | bytes 524288
  53.3 0.3 copy-done
  53.7 0.7 %copy.12 = bf16[128,2,512]{2,1,0:T(2,128)(2,1)} copy(bf16[128,2,512]{2,1,0:T(2,128)(2,1)S(1)} %copy-done) | data formatting | bytes 524288
Async XLA Ops:
  50.8 1.8 %copy-start.1 = (bf16[128,2,512]{2,1,0:T(2,128)(2,1)S(1)}, bf16[128,2,512]{2,1,0:T(2,128)(2,1)}, u32[]{:S(2)}) copy-start(bf16[128,2,512]{2,1,0:T(2,128)(2,1)} %get-tuple-element.16) | copy-start | bytes 786436
  52.6 1.0 %copy-start = (bf16[128,2,512]{2,1,0:T(2,128)(2,1)S(1)}, bf16[128,2,512]{2,1,0:T(2,128)(2,1)}, u32[]{:S(2)}) copy-start(bf16[128,2,512]{2,1,0:T(2,128)(2,1)} %get-tuple-element.17) | copy-start | bytes 786436

commit v7 on v6

--- a/solution.py
+++ b/solution.py
@@ -326,15 +326,6 @@
             for u in range(srv):
                 dq_out[u] = (dq_t[:, pl.ds(u * wide, wide)] * scale).T.astype(jnp.bfloat16)
                 dq_copy(send, u)
-            for u in range(srv):
-                arrived(att_in.at[u], att_got.at[u])
-                by_row(att_in, att_ref, u)
-
-        @pl.when(i == tiles + LAG - 2)
-        def _():
-            for u in range(srv):
-                arrived(dq_in.at[u], dq_got.at[u])
-                by_row(dq_in, dq_ref, u)
 
         @pl.when(i >= LAG)
         def _():
@@ -366,6 +357,12 @@
     lax.fori_loop(0, tiles + LAG, backward, 0)
 
 
+    for u in range(srv):
+        arrived(att_in.at[u], att_got.at[u])
+        by_row(att_in, att_ref, u)
+    for u in range(srv):
+        arrived(dq_in.at[u], dq_got.at[u])
+        by_row(dq_in, dq_ref, u)
     doc_copies(sent)
     key_copies(sent)
     query_copies(sent)

time: 54.9 us -> 53.1 us (0.967)
  Pallas kernels: 50.2 us -> 48.7 us
    pallas_call x1, Pallas kernels: 50.2 us -> 48.7 us  [local_window(): pl.pallas_call(functools.partial(attend, sizes), out_shape=(jax.ShapeDtyp...]
where the time goes in v7:
time: 53.1 us; the launch traced here: 52.9 us
  Pallas kernels  48.7 us (92%)
  local copies, waits for them, and re-layouts  3.53 us (7%)
  between operations  0.65 us (1%)
    pallas_call x1, Pallas kernels, local_window(): pl.pallas_call(functools.partial(attend, sizes), out_shape=(jax.ShapeDtyp...  48.7 us
    squeeze x1, local copies, waits for them, and re-layouts, local_window(): return (att, dq, kv[0], kv[1])  1.78 us
    unnamed x6, local copies, waits for them, and re-layouts  1.75 us

profile of v7, /device:TPU:13, one launch (start us, length us, event | category | flops | bytes accessed | tf_op | source)
XLA Modules:
  0.0 52.9 jit_solution(12030963004785732861)
XLA Ops:
  0.6 48.7 %shard_map.84 = (bf16[128,2,512]{2,1,0:T(2,128)(2,1)}, bf16[128,2,512]{2,1,0:T(2,128)(2,1)}, bf16[2,80,1024]{2,1,0:T(8,128)(2,1)}) custom-call(bf16[128,2,512]{2,1,0:T(2,128)(2,1)} %q_ref.1, bf16[128,2,512]{2,1,0:T(2,128)(2,1)} %o_ref.1, bf16[320,1024]{1,0:T(8,128)(2,1)} %k_ref.1, bf16[320,1024]{1,0:T(8,128)(2,1)} %v_ref.1, s32[5,128]{1,0:T(8,128)} %bitcast.5), custom_call_target="tpu_custom_call" | custom-call | tf_op jit(solution)/shard_map/pallas_call | solution.py:431
  49.3 0.0 copy-start.1
  49.4 1.8 %slice_bitcast_fusion = (bf16[80,1024]{1,0:T(8,128)(2,1)}, bf16[80,1024]{1,0:T(8,128)(2,1)}) fusion(bf16[2,80,1024]{2,1,0:T(8,128)(2,1)} %get-tuple-element.9), kind=kLoop, calls=%fused_computation | loop fusion | bytes 655360 | tf_op jit(solution)/shard_map/squeeze | solution.py:475
  51.1 0.0 copy-done.1
  51.1 0.0 copy-start
  51.1 0.7 %copy.11 = bf16[128,2,512]{2,1,0:T(2,128)(2,1)} copy(bf16[128,2,512]{2,1,0:T(2,128)(2,1)S(1)} %copy-done.1) | data formatting | bytes 524288
  51.8 0.3 copy-done
  52.2 0.7 %copy.12 = bf16[128,2,512]{2,1,0:T(2,128)(2,1)} copy(bf16[128,2,512]{2,1,0:T(2,128)(2,1)S(1)} %copy-done) | data formatting | bytes 524288
Async XLA Ops:
  49.3 1.8 %copy-start.1 = (bf16[128,2,512]{2,1,0:T(2,128)(2,1)S(1)}, bf16[128,2,512]{2,1,0:T(2,128)(2,1)}, u32[]{:S(2)}) copy-start(bf16[128,2,512]{2,1,0:T(2,128)(2,1)} %get-tuple-element.16) | copy-start | bytes 786436
  51.1 1.0 %copy-start = (bf16[128,2,512]{2,1,0:T(2,128)(2,1)S(1)}, bf16[128,2,512]{2,1,0:T(2,128)(2,1)}, u32[]{:S(2)}) copy-start(bf16[128,2,512]{2,1,0:T(2,128)(2,1)} %get-tuple-element.17) | copy-start | bytes 786436
